TPU v7x, 256 devices: a whole 4x4x8 slice. The times are simulated.
256 devices in a mesh: gx: 16 (over y_hi, x, core), yz: 16 (over z, y_lo).
Axes of the slice: x: 4, y: 4 (y_hi: 2, y_lo: 2; y = y_hi * 2 + y_lo), z: 8, core: 2. Of those that a mesh axis runs over, the one named last changes fastest.
Arguments:
- vectors: float32 [8, 256, 256, 512], P(None, 'gx', 'yz'), may hold values from -4 to 4
- classes: int32 [256, 256, 512], P('gx', 'yz'), may hold values from 0 to 3
- permittivity: float32 [4], replicated, may hold values from 0.01 to 10
Outputs:
- applied: float32 [8, 256, 256, 512], P(None, 'gx', 'yz')
- coarse: float32 [2048, 2048], P('gx', 'yz')
All inputs are finite; a program needn't handle non-finite values.
Results may differ from a plain program's by a relative error of at most 0.000071.
Values sent between devices are 32-bit elements; how exact they have to be, the bound alone decides.
No kernel may reach another device: no remote copies, remote signals or barrier semaphores. Data moves between devices by JAX's collectives and lax.ppermute only.
A program may use at most 64 MiB of HBM per device.

v0:
```python
import jax
import jax.numpy as jnp
from jax import lax
from jax.sharding import PartitionSpec as P


def padded_2(block, sides, width):
    for axis, dim in sides:
        count = lax.axis_size(axis)
        forward = [(i, i + 1) for i in range(count - 1)]
        backward = [(target, source) for source, target in forward]
        low = lax.ppermute(
            lax.slice_in_dim(block, block.shape[dim] - width, None, axis=dim), axis, forward
        )
        high = lax.ppermute(lax.slice_in_dim(block, 0, width, axis=dim), axis, backward)
        block = jnp.concatenate([low, block, high], axis=dim)
    return block


def permit(classes, permittivity):
    onehot = (classes[..., None] == jnp.arange(permittivity.shape[0], dtype=jnp.int32)).astype(
        jnp.float32
    )
    return jnp.sum(onehot * permittivity, axis=-1)


def harmonic(first_value, second_value):
    return 2.0 * first_value * second_value / (first_value + second_value)


def stencil(vectors, epsilon, x_low, x_high, z_low, z_high):
    full_x = jnp.concatenate([x_low, epsilon, x_high], axis=0)
    face_x = harmonic(full_x[:-1], full_x[1:])
    pad_x = jnp.pad(vectors, ((0, 0), (1, 1), (0, 0), (0, 0)))
    applied = face_x[:-1] * (vectors - pad_x[:, :-2]) + face_x[1:] * (vectors - pad_x[:, 2:])
    full_z = jnp.concatenate([z_low, epsilon, z_high], axis=1)
    face_z = harmonic(full_z[:, :-1], full_z[:, 1:])
    pad_z = jnp.pad(vectors, ((0, 0), (0, 0), (1, 1), (0, 0)))
    applied = (
        applied
        + face_z[:, :-1] * (vectors - pad_z[:, :, :-2])
        + face_z[:, 1:] * (vectors - pad_z[:, :, 2:])
    )
    face_y = jnp.pad(harmonic(epsilon[..., :-1], epsilon[..., 1:]), ((0, 0), (0, 0), (1, 1)))
    pad_y = jnp.pad(vectors, ((0, 0), (0, 0), (0, 0), (1, 1)))
    applied = (
        applied
        + face_y[..., :-1] * (vectors - pad_y[..., :-2])
        + face_y[..., 1:] * (vectors - pad_y[..., 2:])
    )
    return applied


def coupling(own_face, own_eps, other_face, other_eps):
    weighted = own_face * harmonic(own_eps, other_eps)
    return -jnp.einsum("kzy,lzy->kl", weighted, other_face, precision=lax.Precision.HIGHEST)


def place_blocks(blocks, targets, first_column, width):
    local = targets - first_column
    onehot = (local[..., None] == jnp.arange(width, dtype=jnp.int32)).astype(jnp.float32)
    placed = jnp.einsum("rmkl,rms->rksl", blocks, onehot, precision=lax.Precision.HIGHEST)
    return placed.reshape(blocks.shape[0] * blocks.shape[2], width * blocks.shape[3])


def shards(vectors, classes, permittivity):
    vector_count = vectors.shape[0]
    epsilon = permit(classes, permittivity)
    stacked = jnp.concatenate([vectors, epsilon[None]], axis=0)
    padded = padded_2(stacked, (("gx", 1), ("yz", 2)), 1)
    x_low = padded[:, 0, 1:-1]
    x_high = padded[:, -1, 1:-1]
    z_low = padded[:, 1:-1, 0]
    z_high = padded[:, 1:-1, -1]
    applied = stencil(
        vectors,
        epsilon,
        x_low[vector_count][None],
        x_high[vector_count][None],
        z_low[vector_count][:, None],
        z_high[vector_count][:, None],
    )
    upper_x = coupling(vectors[:, -1], epsilon[-1], x_high[:vector_count], x_high[vector_count])
    lower_x = coupling(vectors[:, 0], epsilon[0], x_low[:vector_count], x_low[vector_count])
    upper_z = coupling(
        vectors[:, :, -1], epsilon[:, -1], z_high[:vector_count], z_high[vector_count]
    )
    lower_z = coupling(vectors[:, :, 0], epsilon[:, 0], z_low[:vector_count], z_low[vector_count])
    self_block = jnp.einsum("kxzy,lxzy->kl", vectors, applied, precision=lax.Precision.HIGHEST)
    scaling = 1.0 / (vectors.shape[2] * vectors.shape[3])
    blocks = jnp.stack([self_block, upper_x, lower_x, upper_z, lower_z]) * scaling
    tile_count = lax.axis_size("yz")
    order_total = tile_count * lax.axis_size("gx")
    slab_index = lax.axis_index("gx")
    tile_index = lax.axis_index("yz")
    offsets = jnp.array([0, tile_count, -tile_count, 1, -1], jnp.int32)
    own_ids = slab_index * tile_count + jnp.reshape(tile_index, (1,))
    row_slab = place_blocks(
        blocks[None], jnp.mod(own_ids[:, None] + offsets, order_total), 0, order_total
    )
    coarse = lax.all_to_all(row_slab, "yz", split_axis=1, concat_axis=0, tiled=True)
    return (applied, coarse)


def solution(mesh):
    return jax.shard_map(
        shards,
        mesh=mesh,
        in_specs=(P(None, "gx", "yz", None), P("gx", "yz", None), P()),
        out_specs=(P(None, "gx", "yz", None), P("gx", "yz")),
        check_vma=False,
    )
```

profile of v0, /device:TPU:16, one launch (start us, length us, event | category | flops | bytes accessed | tf_op | source)
XLA Modules:
  0.0 116.0 jit_solution(4873791190578419026)
XLA Ops:
  0.6 1.4 %select_reduce_fusion = f32[16,16,512]{2,1,0:T(8,128)S(1)} fusion(f32[4]{0:T(128)} %param.6, s32[16,16,512]{2,1,0:T(8,128)} %param.5), kind=kLoop, calls=%fused_computation.27 | loop fusion | flops 1441792 | bytes 1048592 | tf_op jit(solution)/shard_map/reduce_sum | solution.py:24
  2.4 7.7 %copy_dynamic-update-slice_fusion = f32[9,16,16,512]{3,0,2,1:T(8,128)} fusion(f32[8,16,16,512]{3,2,1,0:T(8,128)} %param.4), kind=kLoop, calls=%fused_computation.26 | loop fusion | bytes 8388608
  10.1 11.4 %dynamic-update-slice.1 = f32[9,16,16,512]{3,0,2,1:T(8,128)} dynamic-update-slice(f32[9,16,16,512]{3,0,2,1:T(8,128)} %copy_dynamic-update-slice_fusion, f32[1,16,16,512]{3,0,2,1:T(1,128)S(1)} %broadcast_in_dim.2, s32[]{} %constant.53, s32[]{} %constant.52, s32[]{} %constant.52, s32[]{} %constant.52) | dynamic-update-slice | bytes 1048580 | tf_op jit(solution)/shard_map/concatenate | solution.py:69
  21.5 1.3 %fusion.48 = (f32[9,1,16,512]{3,0,2,1:T(8,128)S(1)}, f32[9,1,16,512]{3,0,2,1:T(8,128)S(1)}) fusion(f32[9,16,16,512]{3,0,2,1:T(8,128)} %dynamic-update-slice.1), kind=kLoop, calls=%fused_computation.96 | loop fusion | bytes 1179648 | tf_op jit(solution)/shard_map/slice | solution.py:13
  22.7 1.9 %collective-permute-start = (f32[9,1,16,512]{3,0,2,1:T(8,128)S(1)}, f32[9,1,16,512]{3,0,2,1:T(8,128)S(1)}, u32[]{:S(2)}, u32[]{:S(2)}) collective-permute-start(f32[9,1,16,512]{3,0,2,1:T(8,128)S(1)} %get-tuple-element.4), channel_id=1, source_target_pairs={{0,16},{16,32},{32,48},{48,64},{64,80},{80,96},{96,112},{112,128},... | collective-permute-start | bytes 884744 | tf_op jit(solution)/shard_map/ppermute | solution.py:12
  24.7 7.3 %collective-permute-start.1 = (f32[9,1,16,512]{3,0,2,1:T(8,128)S(1)}, f32[9,1,16,512]{3,0,2,1:T(8,128)S(1)}, u32[]{:S(2)}, u32[]{:S(2)}) collective-permute-start(f32[9,1,16,512]{3,0,2,1:T(8,128)S(1)} %get-tuple-element.5), channel_id=1, source_target_pairs={{16,0},{32,16},{48,32},{64,48},{80,64},{96,80},{112,96},{128,112},... | collective-permute-start | bytes 884744 | tf_op jit(solution)/shard_map/ppermute | solution.py:15
  31.9 0.7 fusion.53
  33.4 3.6 %fusion.49 = (f32[8,16,1,512]{3,2,1,0:T(1,128)}, f32[8,16,1,512]{3,2,1,0:T(1,128)}) fusion(f32[8,16,16,512]{3,2,1,0:T(8,128)} %param.4), kind=kLoop, calls=%fused_computation.97 | loop fusion | bytes 1048576 | tf_op jit(solution)/shard_map/slice | solution.py:88
  37.1 1.6 %collective-permute-done.1 = f32[9,1,16,512]{3,0,2,1:T(8,128)S(1)} collective-permute-done((f32[9,1,16,512]{3,0,2,1:T(8,128)S(1)}, f32[9,1,16,512]{3,0,2,1:T(8,128)S(1)}, u32[]{:S(2)}, u32[]{:S(2)}) %collective-permute-start.1) | collective-permute-done | bytes 294944 | tf_op jit(solution)/shard_map/ppermute | solution.py:15
  38.6 2.2 %pad_maximum_fusion.4 = (f32[9,18,1,512]{3,0,2,1:T(8,128)S(1)}, f32[9,18,1,512]{3,0,2,1:T(8,128)}) fusion(f32[9,1,16,512]{3,0,2,1:T(8,128)S(1)} %collective-permute-done.1, f32[9,16,16,512]{3,0,2,1:T(8,128)} %dynamic-update-slice.1, f32[9,1,16,512]{3,0,2,1:T(8,128)S(1)} %collective-permute-done), kind=kLoop, calls=%fused_computation.50 | loop fusion | flops 331776 | bytes 5971968 | tf_op jit(solution)/shard_map/slice | solution.py:13
  41.0 4.0 %collective-permute-start.2 = (f32[9,18,1,512]{3,1,2,0:T(8,128)S(1)}, f32[9,18,1,512]{3,1,2,0:T(8,128)}, u32[]{:S(2)}, u32[]{:S(2)}) collective-permute-start(f32[9,18,1,512]{3,1,2,0:T(8,128)S(1)} %copy.137), channel_id=1, source_target_pairs={{0,1},{1,2},{2,3},{3,4},{4,5},{5,6},{6,7},{7,8},{8,9},{9,10},{10,1... | collective-permute-start | bytes 995336 | tf_op jit(solution)/shard_map/ppermute | solution.py:12
  45.0 1.3 %collective-permute-start.3 = (f32[9,18,1,512]{3,0,2,1:T(8,128)}, f32[9,18,1,512]{3,0,2,1:T(8,128)}, u32[]{:S(2)}, u32[]{:S(2)}) collective-permute-start(f32[9,18,1,512]{3,0,2,1:T(8,128)} %get-tuple-element.3), channel_id=1, source_target_pairs={{1,0},{2,1},{3,2},{4,3},{5,4},{6,5},{7,6},{8,7},{9,8},{10,9},{11,1... | collective-permute-start | bytes 995336 | tf_op jit(solution)/shard_map/ppermute | solution.py:15
  46.5 1.1 bitcast_multiply_fusion
  47.6 0.7 fusion.30
  48.3 0.7 copy.126
  49.0 0.7 fusion.32
  49.7 0.8 copy.125
  50.6 0.9 fusion.52
  51.5 9.0 %collective-permute-done.3 = f32[9,18,1,512]{3,0,2,1:T(8,128)} collective-permute-done((f32[9,18,1,512]{3,0,2,1:T(8,128)}, f32[9,18,1,512]{3,0,2,1:T(8,128)}, u32[]{:S(2)}, u32[]{:S(2)}) %collective-permute-start.3) | collective-permute-done | bytes 331808 | tf_op jit(solution)/shard_map/ppermute | solution.py:15
  60.5 1.0 fusion.51
  61.5 3.3 %collective-permute-done.2 = f32[9,18,1,512]{3,1,2,0:T(8,128)} collective-permute-done((f32[9,18,1,512]{3,1,2,0:T(8,128)S(1)}, f32[9,18,1,512]{3,1,2,0:T(8,128)}, u32[]{:S(2)}, u32[]{:S(2)}) %collective-permute-start.2) | collective-permute-done | bytes 331808 | tf_op jit(solution)/shard_map/ppermute | solution.py:12
  64.7 0.8 fusion.42
  65.6 1.1 fusion.33
  66.7 1.0 slice_bitcast_fusion
  67.7 0.8 fusion.26
  68.6 1.0 slice_bitcast_fusion.9
  70.2 0.7 copy-done
  70.9 5.8 %fusion.6 = f32[8,16,16,512]{3,2,1,0:T(8,128)S(1)} fusion(f32[8,16,16,512]{3,2,1,0:T(8,128)S(1)} %copy-done, f32[16,16,512]{2,1,0:T(8,128)S(1)} %get-tuple-element.21, f32[16,16,512]{2,1,0:T(8,128)S(1)} %get-tuple-element.20, f32[16,16,512]{2,1,0:T(8,128)S(1)} %get-tuple-element.22, f32[16,16,512]{2,1,0:T(8,128)S(1)} %get-tuple-element.23, ...), kind=kLoop, calls=%fused_computation.12 | loop fusion | flops 17825792 | bytes 11534336 | tf_op jit(solution)/shard_map/add | solution.py:47
  76.6 2.0 %copy-done.1 = f32[8,16,16,512]{3,2,1,0:T(8,128)} copy-done((f32[8,16,16,512]{3,2,1,0:T(8,128)}, f32[8,16,16,512]{3,2,1,0:T(8,128)S(1)}, u32[]{:S(2)}) %copy-start.1) | copy-done | bytes 4194328
  78.7 11.7 %fusion.20 = f32[1,8,8]{1,2,0:T(8,128)S(1)} fusion(f32[8,16,16,512]{3,2,1,0:T(8,128)S(1)} %copy-done, f32[8,16,16,512]{3,2,1,0:T(8,128)S(1)} %fusion.6), kind=kOutput, calls=%fused_computation.30 | convolution fusion | flops 100663296 | bytes 8388864 | tf_op jit(solution)/shard_map/kxzy,lxzy->kl/dot_general | solution.py:89
  90.5 1.7 %fusion.28 = f32[1,8,8]{2,1,0:T(8,128)S(1)} fusion(f32[9,18,1,512]{3,0,2,1:T(8,128)} %collective-permute-done.3, f32[8,16,512]{2,1,0:T(8,128)S(1)} %get-tuple-element.25), kind=kOutput, calls=%fused_computation.36 | convolution fusion | flops 6291520 | bytes 524544 | tf_op jit(solution)/shard_map/kzy,lzy->kl/dot_general | solution.py:56
  93.5 21.9 %all_to_all.19 = f32[8,16,128]{2,0,1:T(8,128)S(1)} all-to-all(f32[8,16,128]{2,0,1:T(8,128)S(1)} %copy.130), channel_id=1, replica_groups=mesh['gx'=16,'yz'=16] {'yz'}, dimensions={1} | all-to-all | bytes 131072 | tf_op jit(solution)/shard_map/all_to_all | solution.py:101
  (42 shorter events, 4.5 us)
Async XLA Ops:
  10.1 23.4 %copy-start.7 = (s32[5]{0:T(128)S(1)}, s32[5]{0:T(128)}, u32[]{:S(2)}) copy-start(s32[5]{0:T(128)} %constant.38.clone) | copy-start | bytes 64
  22.7 14.3 %collective-permute-start = (f32[9,1,16,512]{3,0,2,1:T(8,128)S(1)}, f32[9,1,16,512]{3,0,2,1:T(8,128)S(1)}, u32[]{:S(2)}, u32[]{:S(2)}) collective-permute-start(f32[9,1,16,512]{3,0,2,1:T(8,128)S(1)} %get-tuple-element.4), channel_id=1, source_target_pairs={{0,16},{16,32},{32,48},{48,64},{64,80},{80,96},{96,112},{112,128},... | collective-permute-start | bytes 884744 | tf_op jit(solution)/shard_map/ppermute | solution.py:12
  24.7 13.9 %collective-permute-start.1 = (f32[9,1,16,512]{3,0,2,1:T(8,128)S(1)}, f32[9,1,16,512]{3,0,2,1:T(8,128)S(1)}, u32[]{:S(2)}, u32[]{:S(2)}) collective-permute-start(f32[9,1,16,512]{3,0,2,1:T(8,128)S(1)} %get-tuple-element.5), channel_id=1, source_target_pairs={{16,0},{32,16},{48,32},{64,48},{80,64},{96,80},{112,96},{128,112},... | collective-permute-start | bytes 884744 | tf_op jit(solution)/shard_map/ppermute | solution.py:15
  37.0 9.3 %copy-start.4 = (f32[1,16,512]{2,1,0:T(8,128)S(1)}, f32[1,16,512]{2,1,0:T(8,128)}, u32[]{:S(2)}) copy-start(f32[1,16,512]{2,1,0:T(8,128)} %get-tuple-element.18) | copy-start | bytes 98308
  37.1 9.4 %copy-start.3 = (f32[1,16,512]{2,1,0:T(8,128)S(1)}, f32[1,16,512]{2,1,0:T(8,128)}, u32[]{:S(2)}) copy-start(f32[1,16,512]{2,1,0:T(8,128)} %get-tuple-element.19) | copy-start | bytes 98308
  40.8 20.7 %copy-start.2 = (f32[16,1,512]{2,1,0:T(1,128)S(1)}, f32[16,1,512]{2,1,0:T(1,128)}, u32[]{:S(2)}) copy-start(f32[16,1,512]{2,1,0:T(1,128)} %get-tuple-element.17) | copy-start | bytes 98308
  41.0 23.8 %collective-permute-start.2 = (f32[9,18,1,512]{3,1,2,0:T(8,128)S(1)}, f32[9,18,1,512]{3,1,2,0:T(8,128)}, u32[]{:S(2)}, u32[]{:S(2)}) collective-permute-start(f32[9,18,1,512]{3,1,2,0:T(8,128)S(1)} %copy.137), channel_id=1, source_target_pairs={{0,1},{1,2},{2,3},{3,4},{4,5},{5,6},{6,7},{7,8},{8,9},{9,10},{10,1... | collective-permute-start | bytes 995336 | tf_op jit(solution)/shard_map/ppermute | solution.py:12
  45.0 15.5 %collective-permute-start.3 = (f32[9,18,1,512]{3,0,2,1:T(8,128)}, f32[9,18,1,512]{3,0,2,1:T(8,128)}, u32[]{:S(2)}, u32[]{:S(2)}) collective-permute-start(f32[9,18,1,512]{3,0,2,1:T(8,128)} %get-tuple-element.3), channel_id=1, source_target_pairs={{1,0},{2,1},{3,2},{4,3},{5,4},{6,5},{7,6},{8,7},{9,8},{10,9},{11,1... | collective-permute-start | bytes 995336 | tf_op jit(solution)/shard_map/ppermute | solution.py:15
  68.6 2.2 %copy-start = (f32[8,16,16,512]{3,2,1,0:T(8,128)S(1)}, f32[8,16,16,512]{3,2,1,0:T(8,128)}, u32[]{:S(2)}) copy-start(f32[8,16,16,512]{3,2,1,0:T(8,128)} %param.4) | copy-start | bytes 12582916
  76.6 2.0 %copy-start.1 = (f32[8,16,16,512]{3,2,1,0:T(8,128)}, f32[8,16,16,512]{3,2,1,0:T(8,128)S(1)}, u32[]{:S(2)}) copy-start(f32[8,16,16,512]{3,2,1,0:T(8,128)S(1)} %fusion.6) | copy-start | bytes 12582916
  78.7 13.6 %copy-start.5 = (f32[1,8,8]{0,2,1:T(8,128)S(1)}, f32[1,8,8]{0,2,1:T(8,128)}, u32[]{:S(2)}) copy-start(f32[1,8,8]{0,2,1:T(8,128)} %copy.126) | copy-start | bytes 772
  78.7 13.6 %copy-start.6 = (f32[1,8,8]{0,2,1:T(8,128)S(1)}, f32[1,8,8]{0,2,1:T(8,128)}, u32[]{:S(2)}) copy-start(f32[1,8,8]{0,2,1:T(8,128)} %copy.125) | copy-start | bytes 772
where the time goes:
time: 117 us; the launch traced here: 116 us
  local copies, waits for them, and re-layouts  36.2 us (31%)
  blocking collectives  21.9 us (19%)
  matrix products  15.8 us (14%)
  starting transfers between devices  14.4 us (12%)
  waiting for transfers between devices  13.8 us (12%)
  other arithmetic  12.9 us (11%)
    all_to_all x1, blocking collectives, shards(): lax.all_to_all(row_slab, 'yz', split_axis=1, concat_axis=0, tiled=True)  21.9 us
    dot_general x1, matrix products, shards(): jnp.einsum('kxzy,lxzy->kl', vectors, applied, precision=lax.Precision.HIG...  11.7 us
    concatenate x1, local copies, waits for them, and re-layouts, shards(): stacked = jnp.concatenate([vectors, epsilon[None]], axis=0)  11.4 us
    unnamed x21, local copies, waits for them, and re-layouts  11.2 us
    ppermute x2, waiting for transfers between devices, padded_2(): lax.ppermute(lax.slice_in_dim(block, 0, width, axis=dim), axis, backward)  10.6 us
    ppermute x2, starting transfers between devices, padded_2(): lax.ppermute(lax.slice_in_dim(block, 0, width, axis=dim), axis, backward)  8.54 us
    ppermute x2, starting transfers between devices, padded_2(): lax.ppermute(lax.slice_in_dim(block, block.shape[dim] - width, None, axis...  5.9 us
    add x1, other arithmetic, stencil(): applied + face_y[..., :-1] * (vectors - pad_y[..., :-2])  5.76 us
  transfers between devices with their start and end apart: 4, of which 3 were waited for; matrix products, arithmetic and copies ran while one was open for 10% of the time, Pallas kernels for 0%

commit v1 on v0

v1 whole, which is shorter than its diff:
```python
import functools
import jax
import jax.numpy as jnp
from jax import lax
from jax.experimental import pallas as pl
from jax.experimental.pallas import tpu as pltpu
from jax.sharding import PartitionSpec as P

F32 = jnp.float32
BF16 = jnp.bfloat16


def harmonic(first_value, second_value):
    return 2.0 * first_value * second_value / (first_value + second_value)


def permit(classes, table):
    value = jnp.where(classes == 0, table[0], 0.0)
    for index in range(1, table.shape[0]):
        value = jnp.where(classes == index, table[index], value)
    return value


def split(rows):
    high = rows.astype(BF16)
    low = (rows - high.astype(F32)).astype(BF16)
    return jnp.concatenate([high, low], axis=0)


def products(left, right):
    return lax.dot_general(left, right, (((1,), (1,)), ((), ())), preferred_element_type=F32)


def fold(full, count, points):
    size = count * points
    total = (full[:size, :size] + full[:size, size:]) + (full[size:, :size] + full[size:, size:])
    row = lax.broadcasted_iota(jnp.int32, (size, size), 0)
    column = lax.broadcasted_iota(jnp.int32, (size, size), 1)
    total = jnp.where(lax.rem(row, points) == lax.rem(column, points), total, 0.0)
    return jnp.sum(total.reshape(count, points, size), axis=1)


def faces_kernel(table, vectors, classes, x_high, x_low, z_high, z_low, held, values, sems):
    count, cells_x, cells_z, _ = vectors.shape
    copies = [
        pltpu.make_async_copy(vectors.at[:, :, cells_z - 1], z_high.at[0:count], sems.at[0]),
        pltpu.make_async_copy(vectors.at[:, cells_x - 1], x_high.at[0:count], sems.at[1]),
        pltpu.make_async_copy(vectors.at[:, 0], x_low.at[0:count], sems.at[2]),
    ]
    layers = [
        pltpu.make_async_copy(classes.at[:, cells_z - 1], held.at[0], sems.at[3]),
        pltpu.make_async_copy(classes.at[cells_x - 1], held.at[1], sems.at[4]),
        pltpu.make_async_copy(classes.at[0], held.at[2], sems.at[5]),
        pltpu.make_async_copy(classes.at[:, 0], held.at[3], sems.at[6]),
    ]
    for copy in layers + copies:
        copy.start()
    places = [z_high.at[count], x_high.at[count], x_low.at[count], z_low]
    for index, (layer, place) in enumerate(zip(layers, places)):
        layer.wait()
        values[index] = permit(held[index], table)
        copy = pltpu.make_async_copy(values.at[index], place, sems.at[7 + index])
        copy.start()
        copies.append(copy)
    for copy in copies:
        copy.wait()


def block_kernel(
    chunks, table, vectors, classes, applied, own, z_face, x_sums, z_sums, held, kinds, face_x, result, total, sems
):
    count, cells_x, cells_z, length = vectors.shape
    step = cells_x // chunks
    kind_copy = pltpu.make_async_copy(classes, kinds, sems.at[0])
    kind_copy.start()
    loads, stores = [], []
    for chunk in range(chunks):
        planes = pl.ds(chunk * step, step)
        load = pltpu.make_async_copy(vectors.at[:, planes], held.at[:, planes], sems.at[3 + chunk])
        load.start()
        loads.append(load)
        stores.append(
            pltpu.make_async_copy(result.at[:, planes], applied.at[:, planes], sems.at[3 + chunks + chunk])
        )
    face_copy = pltpu.make_async_copy(vectors.at[:, :, 0], z_face, sems.at[1])
    face_copy.start()
    face_x[0] = jnp.zeros((cells_z, length), F32)
    total[...] = jnp.zeros_like(total)
    row = lax.broadcasted_iota(jnp.int32, (cells_z, length), 0)
    column = lax.broadcasted_iota(jnp.int32, (cells_z, length), 1)
    kind_copy.wait()

    def plane(index, carry):
        before = jnp.maximum(index - 1, 0)
        after = jnp.minimum(index + 1, cells_x - 1)
        value = permit(kinds[index], table)
        value_after = permit(kinds[after], table)
        low_x = face_x[index]
        high_x = jnp.where(index + 1 < cells_x, harmonic(value, value_after), 0.0)
        face_x[index + 1] = high_x
        value_z = pltpu.roll(value, cells_z - 1, 0)
        value_y = pltpu.roll(value, length - 1, 1)
        high_z = jnp.where(row < cells_z - 1, harmonic(value, value_z), 0.0)
        high_y = jnp.where(column < length - 1, harmonic(value, value_y), 0.0)
        for k in range(count):
            here = held[k, index]
            flux = low_x * (here - held[k, before]) + high_x * (here - held[k, after])
            flux_z = high_z * (here - pltpu.roll(here, cells_z - 1, 0))
            flux = flux + (flux_z - pltpu.roll(flux_z, 1, 0))
            flux_y = high_y * (here - pltpu.roll(here, length - 1, 1))
            flux = flux + (flux_y - pltpu.roll(flux_y, 1, 1))
            result[k, index] = flux
        left = split(held[:, index].reshape(count * cells_z, length))
        right = split(result[:, index].reshape(count * cells_z, length))
        total[...] += products(left, right)
        return carry

    loads[0].wait()
    for chunk in range(chunks):
        if chunk + 1 < chunks:
            loads[chunk + 1].wait()
        lax.fori_loop(chunk * step, (chunk + 1) * step, plane, 0)
        stores[chunk].start()
    sides = [
        pltpu.make_async_copy(result.at[:, 0], x_sums.at[0], sems.at[3 + 2 * chunks]),
        pltpu.make_async_copy(result.at[:, cells_x - 1], x_sums.at[1], sems.at[4 + 2 * chunks]),
        pltpu.make_async_copy(result.at[:, :, 0], z_sums.at[0], sems.at[5 + 2 * chunks]),
        pltpu.make_async_copy(result.at[:, :, cells_z - 1], z_sums.at[1], sems.at[6 + 2 * chunks]),
    ]
    for copy in sides:
        copy.start()
    own[...] = fold(total[...], count, cells_z)
    for copy in [face_copy] + sides + stores:
        copy.wait()


def outer_kernel(
    place, applied_in, own, z_face, x_sums, z_sums, x_high, x_low, z_high, z_low,
    from_x_low, from_x_high, from_z_low, from_z_high, applied, blocks, x_new, z_new, sems,
):
    count, cells_x, cells_z, length = applied.shape
    slots, _, width = blocks.shape
    slab, tile = place[0], place[1]
    last_slab, last_tile = place[2], place[3]
    low_x = jnp.where(slab > 0, harmonic(x_low[count], from_x_low[count]), 0.0)
    high_x = jnp.where(slab < last_slab, harmonic(x_high[count], from_x_high[count]), 0.0)
    low_z = jnp.where(tile > 0, harmonic(z_low[...], from_z_low[count]), 0.0)
    high_z = jnp.where(tile < last_tile, harmonic(z_high[count], from_z_high[...]), 0.0)
    flux_near = z_face[...] * low_z
    flux_far = z_high[0:count] * high_z
    z_new[0] = z_sums[0] + flux_near
    z_new[1] = z_sums[1] + flux_far
    z_stores = [
        pltpu.make_async_copy(z_new.at[0], applied.at[:, :, 0], sems.at[0]),
        pltpu.make_async_copy(z_new.at[1], applied.at[:, :, cells_z - 1], sems.at[1]),
    ]
    for copy in z_stores:
        copy.start()
    flux_low = x_low[0:count] * low_x
    flux_high = x_high[0:count] * high_x
    x_new[0] = x_sums[0] + flux_low
    x_new[1] = x_sums[1] + flux_high
    for side, at in ((0, 0), (1, cells_x - 1)):
        x_new[side, :, 0:1, :] += flux_near[:, at : at + 1, :]
        x_new[side, :, cells_z - 1 : cells_z, :] += flux_far[:, at : at + 1, :]

    def rows(block):
        return block.reshape(count * block.shape[1], length)

    left_near, left_far = split(rows(flux_near)), split(rows(flux_far))
    own_z = products(left_near, split(rows(z_face[...]))) + products(left_far, split(rows(z_high[0:count])))
    cross_z = fold(products(left_near, split(rows(from_z_low[0:count]))), count, cells_x)
    for copy in z_stores:
        copy.wait()
    x_stores = [
        pltpu.make_async_copy(x_new.at[0], applied.at[:, 0], sems.at[2]),
        pltpu.make_async_copy(x_new.at[1], applied.at[:, cells_x - 1], sems.at[3]),
    ]
    for copy in x_stores:
        copy.start()
    left_low, left_high = split(rows(flux_low)), split(rows(flux_high))
    own_x = products(left_low, split(rows(x_low[0:count]))) + products(left_high, split(rows(x_high[0:count])))
    cross_low = fold(products(left_low, split(rows(from_x_low[0:count]))), count, cells_z)
    cross_high = fold(products(left_high, split(rows(from_x_high[0:count]))), count, cells_z)
    self_rows = own[...] + fold(own_x, count, cells_z)
    self_z = fold(own_z, count, cells_x)

    scale = 1.0 / (cells_z * length)
    entry = lax.broadcasted_iota(jnp.int32, (count * cells_z, width), 0)
    column = lax.broadcasted_iota(jnp.int32, (count * cells_z, width), 1)
    here = (lax.div(entry, cells_z) + tile * count == column).astype(F32)
    entry = lax.broadcasted_iota(jnp.int32, (count * cells_x, width), 0)
    column = lax.broadcasted_iota(jnp.int32, (count * cells_x, width), 1)
    here_z = (lax.div(entry, cells_x) + tile * count == column).astype(F32)
    before_z = (lax.div(entry, cells_x) + (tile - 1) * count == column).astype(F32)
    highest = lax.Precision.HIGHEST
    stacked = jnp.concatenate([self_rows, -cross_low, -cross_high], axis=0)
    placed = jnp.dot(stacked, here, precision=highest, preferred_element_type=F32) * scale
    placed_z = jnp.dot(
        jnp.concatenate([self_z, -cross_z], axis=1),
        jnp.concatenate([here_z, before_z], axis=0),
        precision=highest,
        preferred_element_type=F32,
    )
    blocks[...] = jnp.zeros_like(blocks)
    blocks[slab] = placed[0:count] + placed_z * scale

    @pl.when(slab > 0)
    def _():
        blocks[slab - 1] = placed[count : 2 * count]

    @pl.when(slab < last_slab)
    def _():
        blocks[slab + 1] = placed[2 * count : 3 * count]

    for copy in x_stores:
        copy.wait()


def finish_kernel(count, tile, coarse):
    size = tile.shape[0]
    row = lax.broadcasted_iota(jnp.int32, (size, size), 0)
    column = lax.broadcasted_iota(jnp.int32, (size, size), 1)
    value = tile[...]
    other = jnp.where(lax.div(row, count) == lax.div(column, count), 0.0, value.T)
    coarse[...] = value + other


def shards(vectors, classes, permittivity):
    count, cells_x, cells_z, length = vectors.shape
    slabs, tiles = lax.axis_size("gx"), lax.axis_size("yz")
    hbm = pl.BlockSpec(memory_space=pltpu.HBM)
    anywhere = pl.BlockSpec(memory_space=pl.ANY)
    smem = pl.BlockSpec(memory_space=pltpu.SMEM)
    vmem = pl.BlockSpec(memory_space=pltpu.VMEM)
    shape = jax.ShapeDtypeStruct
    limit = 24 * 1024 * 1024
    params = pltpu.CompilerParams(vmem_limit_bytes=limit)
    vectors = pltpu.with_memory_space_constraint(vectors, pltpu.HBM)
    classes = pltpu.with_memory_space_constraint(classes, pltpu.HBM)

    x_high, x_low, z_high, z_low = pl.pallas_call(
        faces_kernel,
        out_shape=(
            shape((count + 1, cells_z, length), F32),
            shape((count + 1, cells_z, length), F32),
            shape((count + 1, cells_x, length), F32),
            shape((cells_x, length), F32),
        ),
        in_specs=[smem, hbm, hbm],
        out_specs=(anywhere,) * 4,
        scratch_shapes=[
            pltpu.VMEM((4, cells_z, length), jnp.int32),
            pltpu.VMEM((4, cells_z, length), F32),
            pltpu.SemaphoreType.DMA((11,)),
        ],
        compiler_params=params,
        name="faces",
    )(permittivity, vectors, classes)

    up_x = [(i, (i + 1) % slabs) for i in range(slabs)]
    up_z = [(i, (i + 1) % tiles) for i in range(tiles)]
    down_x = [(target, source) for source, target in up_x]
    down_z = [(target, source) for source, target in up_z]
    from_z_low = lax.ppermute(z_high, "yz", up_z)
    from_x_low = lax.ppermute(x_high, "gx", up_x)
    from_x_high = lax.ppermute(x_low, "gx", down_x)
    from_z_high = lax.ppermute(z_low, "yz", down_z)

    chunks = 4
    applied, own, z_face, x_sums, z_sums = pl.pallas_call(
        functools.partial(block_kernel, chunks),
        out_shape=(
            pltpu.HBM(vectors.shape, F32),
            shape((count, count * cells_z), F32),
            shape((count, cells_x, length), F32),
            shape((2, count, cells_z, length), F32),
            shape((2, count, cells_x, length), F32),
        ),
        in_specs=[smem, hbm, hbm],
        out_specs=(hbm, vmem, anywhere, anywhere, anywhere),
        scratch_shapes=[
            pltpu.VMEM(vectors.shape, F32),
            pltpu.VMEM(classes.shape, jnp.int32),
            pltpu.VMEM((cells_x + 1, cells_z, length), F32),
            pltpu.VMEM(vectors.shape, F32),
            pltpu.VMEM((2 * count * cells_z, 2 * count * cells_z), F32),
            pltpu.SemaphoreType.DMA((7 + 2 * chunks,)),
        ],
        compiler_params=params,
        cost_estimate=pl.CostEstimate(flops=5_000_000_000, bytes_accessed=20_000_000, transcendentals=0),
        name="block",
    )(permittivity, vectors, classes)

    place = jnp.stack(
        [lax.axis_index("gx"), lax.axis_index("yz"), jnp.int32(slabs - 1), jnp.int32(tiles - 1)]
    ).astype(jnp.int32)
    applied, blocks = pl.pallas_call(
        outer_kernel,
        out_shape=(pltpu.HBM(vectors.shape, F32), shape((tiles, count, count * slabs), F32)),
        in_specs=[smem, hbm] + [vmem] * 12,
        out_specs=(hbm, vmem),
        scratch_shapes=[
            pltpu.VMEM((2, count, cells_z, length), F32),
            pltpu.VMEM((2, count, cells_x, length), F32),
            pltpu.SemaphoreType.DMA((4,)),
        ],
        input_output_aliases={1: 0},
        compiler_params=params,
        name="outer",
    )(
        place, applied, own, z_face, x_sums, z_sums, x_high, x_low, z_high, z_low,
        from_x_low, from_x_high, from_z_low, from_z_high,
    )
    tile = lax.all_to_all(blocks, "yz", split_axis=0, concat_axis=0, tiled=True)
    tile = tile.reshape(tiles * count, count * slabs)
    coarse = pl.pallas_call(
        functools.partial(finish_kernel, count),
        out_shape=shape(tile.shape, F32),
        in_specs=[vmem],
        out_specs=vmem,
        compiler_params=params,
        name="finish",
    )(tile)
    return (applied, coarse)


def solution(mesh):
    return jax.shard_map(
        shards,
        mesh=mesh,
        in_specs=(P(None, "gx", "yz", None), P("gx", "yz", None), P()),
        out_specs=(P(None, "gx", "yz", None), P("gx", "yz")),
        check_vma=False,
    )
```

time: 117 us -> 44 us (0.38)
  local copies, waits for them, and re-layouts: 36.2 us -> 0.65 us
  Pallas kernels: 0 us -> 15.9 us
  matrix products: 15.8 us -> 0 us
  waiting for transfers between devices: 13.8 us -> 0.01 us
  other arithmetic: 12.9 us -> 0.08 us
  blocking collectives: 21.9 us -> 14.5 us
  starting transfers between devices: 14.4 us -> 12 us
    pallas_call x0 -> x4, Pallas kernels: none -> 15.9 us  [the longest x1 11 us: shards(): pl.pallas_call(functools.partial(block_kernel, chunks), out_shape=(pltpu....]
    dot_general x5 -> x0, matrix products: 15.6 us -> none  [the longest x1 11.7 us: shards(): jnp.einsum('kxzy,lxzy->kl', vectors, applied, precision=lax.Precision.HIG...]
    ppermute x4, waiting for transfers between devices: 13.8 us -> 0.01 us  [the longest x1 0.01 us: shards(): from_z_low = lax.ppermute(z_high, 'yz', up_z)]
    concatenate x1 -> x0, local copies, waits for them, and re-layouts: 11.4 us -> none  [shards(): stacked = jnp.concatenate([vectors, epsilon[None]], axis=0)]
    unnamed x21 -> x4, local copies, waits for them, and re-layouts: 11.2 us -> 0.65 us
    slice x12 -> x0, local copies, waits for them, and re-layouts: 9.41 us -> none  [the longest x1 3.61 us: shards(): vectors[:, :, 0]]
    all_to_all x1, blocking collectives: 21.9 us -> 14.5 us  [shards(): tile = lax.all_to_all(blocks, 'yz', split_axis=0, concat_axis=0, tiled=True)]
    add x1 -> x0, other arithmetic: 5.76 us -> none  [stencil(): applied + face_y[..., :-1] * (vectors - pad_y[..., :-2])]
  transfers between devices with their start and end apart: 4 -> 4, of which waited for: 3 -> 0; matrix products, arithmetic and copies ran while one was open for 10% -> 0% of each run, Pallas kernels for 0% -> 25%
where the time goes in v1:
time: 44 us; the launch traced here: 43.8 us
  Pallas kernels  15.9 us (36%)
  blocking collectives  14.5 us (33%)
  starting transfers between devices  12 us (27%)
  between operations  0.69 us (2%)
  local copies, waits for them, and re-layouts  0.65 us (1%)
    all_to_all x1, blocking collectives, shards(): tile = lax.all_to_all(blocks, 'yz', split_axis=0, concat_axis=0, tiled=True)  14.5 us
    pallas_call x1, Pallas kernels, shards(): pl.pallas_call(functools.partial(block_kernel, chunks), out_shape=(pltpu....  11 us
    ppermute x1, starting transfers between devices, shards(): from_z_high = lax.ppermute(z_low, 'yz', down_z)  6.65 us
    ppermute x1, starting transfers between devices, shards(): from_x_high = lax.ppermute(x_low, 'gx', down_x)  5.36 us
    pallas_call x1, Pallas kernels, shards(): pl.pallas_call(outer_kernel, out_shape=(pltpu.HBM(vectors.shape, F32), sh...  2.27 us
    pallas_call x1, Pallas kernels, shards(): pl.pallas_call(faces_kernel, out_shape=(shape((count + 1, cells_z, length...  1.86 us
  transfers between devices with their start and end apart: 4, of which 0 were waited for; matrix products, arithmetic and copies ran while one was open for 0% of the time, Pallas kernels for 25%

profile of v1, /device:TPU:16, one launch (start us, length us, event | category | flops | bytes accessed | tf_op | source)
XLA Modules:
  0.0 43.8 jit_solution(15862700770151952485)
XLA Ops:
  0.6 0.0 copy-start
  0.6 0.6 %copy-done = f32[4]{0:T(128)S(1)} copy-done((f32[4]{0:T(128)S(1)}, f32[4]{0:T(128)}, u32[]{:S(2)}) %copy-start) | copy-done | bytes 40
  1.3 0.0 copy-start.1
  1.3 1.9 %faces.1 = (f32[9,16,512]{2,1,0:T(8,128)S(1)}, f32[9,16,512]{2,1,0:T(8,128)S(1)}, f32[9,16,512]{2,1,0:T(8,128)S(1)}, f32[16,512]{1,0:T(8,128)S(1)}) custom-call(f32[4]{0:T(128)S(1)} %copy-done, f32[8,16,16,512]{3,2,1,0:T(8,128)} %vectors.3, s32[16,16,512]{2,1,0:T(8,128)} %classes.3), custom_call_target="tpu_custom_call" | custom-call | tf_op jit(solution)/shard_map/faces/pallas_call | solution.py:242
  3.2 6.7 %collective-permute-start.3 = (f32[16,512]{1,0:T(8,128)S(1)}, f32[16,512]{1,0:T(8,128)S(1)}, u32[]{:S(2)}, u32[]{:S(2)}) collective-permute-start(f32[16,512]{1,0:T(8,128)S(1)} %get-tuple-element.21.z_low), channel_id=1, source_target_pairs={{1,0},{2,1},{3,2},{4,3},{5,4},{6,5},{7,6},{8,7},{9,8},{10,9},{11,1... | collective-permute-start | bytes 98312 | tf_op jit(solution)/shard_map/ppermute | solution.py:268
  9.8 0.0 collective-permute-start
  9.8 5.4 %collective-permute-start.1 = (f32[9,16,512]{2,1,0:T(8,128)S(1)}, f32[9,16,512]{2,1,0:T(8,128)S(1)}, u32[]{:S(2)}, u32[]{:S(2)}) collective-permute-start(f32[9,16,512]{2,1,0:T(8,128)S(1)} %get-tuple-element.19.x_low), channel_id=1, source_target_pairs={{16,0},{32,16},{48,32},{64,48},{80,64},{96,80},{112,96},{128,112},... | collective-permute-start | bytes 884744 | tf_op jit(solution)/shard_map/ppermute | solution.py:267
  15.2 0.0 collective-permute-start.2
  15.2 0.0 copy-done.1
  15.2 11.0 %block.1 = (f32[8,16,16,512]{3,2,1,0:T(8,128)}, f32[8,128]{1,0:T(8,128)S(1)}, f32[8,16,512]{2,1,0:T(8,128)S(1)}, f32[2,8,16,512]{3,2,1,0:T(8,128)S(1)}, f32[2,8,16,512]{3,2,1,0:T(8,128)S(1)}) custom-call(f32[4]{0:T(128)S(1)} %copy-done.1, f32[8,16,16,512]{3,2,1,0:T(8,128)} %vectors.3, s32[16,16,512]{2,1,0:T(8,128)} %classes.3), custom_call_target="tpu_custom_call" | custom-call | flops 5000000000 | bytes 20000000 | tf_op jit(solution)/shard_map/block/pallas_call | solution.py:271
  26.2 0.1 pad_add_fusion.place
  26.3 0.0 collective-permute-done.3.from_z_high
  26.3 0.0 collective-permute-done.from_x_low
  26.3 0.0 collective-permute-done.1.from_x_high
  26.3 0.0 collective-permute-done.2.from_z_low
  26.3 2.3 %outer.1 = (f32[8,16,16,512]{3,2,1,0:T(8,128)}, f32[16,8,128]{2,1,0:T(8,128)S(1)}) custom-call(s32[4]{0:T(128)S(1)} %pad_add_fusion.place, f32[8,16,16,512]{3,2,1,0:T(8,128)} %get-tuple-element.13.applied_in, f32[8,128]{1,0:T(8,128)S(1)} %get-tuple-element.14.own, f32[8,16,512]{2,1,0:T(8,128)S(1)} %get-tuple-element.15.z_face, ...), custom_call_target="tpu_custom_call", output_to_operand_aliasing={{0}: (1, {})} | custom-call | tf_op jit(solution)/shard_map/outer/pallas_call | solution.py:298
  28.6 14.5 %all_to_all.5 = f32[16,8,128]{2,1,0:T(8,128)S(1)} all-to-all(f32[16,8,128]{2,1,0:T(8,128)S(1)} %get-tuple-element.23), channel_id=1, replica_groups=mesh['gx'=16,'yz'=16] {'yz'}, dimensions={0} | all-to-all | bytes 131072 | tf_op jit(solution)/shard_map/all_to_all | solution.py:315
  43.1 0.7 %finish.1 = f32[128,128]{1,0:T(8,128)} custom-call(f32[128,128]{1,0:T(8,128)S(1)} %bitcast.3), custom_call_target="tpu_custom_call" | custom-call | tf_op jit(solution)/shard_map/finish/pallas_call | solution.py:317
  (1 shorter events, 0.0 us)
Async XLA Ops:
  0.6 0.7 %copy-start = (f32[4]{0:T(128)S(1)}, f32[4]{0:T(128)}, u32[]{:S(2)}) copy-start(f32[4]{0:T(128)} %table.3) | copy-start | bytes 52
  1.3 13.9 %copy-start.1 = (f32[4]{0:T(128)S(1)}, f32[4]{0:T(128)}, u32[]{:S(2)}) copy-start(f32[4]{0:T(128)} %table.3) | copy-start | bytes 52
  3.2 23.2 %collective-permute-start.3 = (f32[16,512]{1,0:T(8,128)S(1)}, f32[16,512]{1,0:T(8,128)S(1)}, u32[]{:S(2)}, u32[]{:S(2)}) collective-permute-start(f32[16,512]{1,0:T(8,128)S(1)} %get-tuple-element.21.z_low), channel_id=1, source_target_pairs={{1,0},{2,1},{3,2},{4,3},{5,4},{6,5},{7,6},{8,7},{9,8},{10,9},{11,1... | collective-permute-start | bytes 98312 | tf_op jit(solution)/shard_map/ppermute | solution.py:268
  9.8 16.5 %collective-permute-start = (f32[9,16,512]{2,1,0:T(8,128)S(1)}, f32[9,16,512]{2,1,0:T(8,128)S(1)}, u32[]{:S(2)}, u32[]{:S(2)}) collective-permute-start(f32[9,16,512]{2,1,0:T(8,128)S(1)} %get-tuple-element.18.x_high), channel_id=1, source_target_pairs={{0,16},{16,32},{32,48},{48,64},{64,80},{80,96},{96,112},{112,128},... | collective-permute-start | bytes 884744 | tf_op jit(solution)/shard_map/ppermute | solution.py:266
  9.8 16.5 %collective-permute-start.1 = (f32[9,16,512]{2,1,0:T(8,128)S(1)}, f32[9,16,512]{2,1,0:T(8,128)S(1)}, u32[]{:S(2)}, u32[]{:S(2)}) collective-permute-start(f32[9,16,512]{2,1,0:T(8,128)S(1)} %get-tuple-element.19.x_low), channel_id=1, source_target_pairs={{16,0},{32,16},{48,32},{64,48},{80,64},{96,80},{112,96},{128,112},... | collective-permute-start | bytes 884744 | tf_op jit(solution)/shard_map/ppermute | solution.py:267
  15.2 11.2 %collective-permute-start.2 = (f32[9,16,512]{2,1,0:T(8,128)S(1)}, f32[9,16,512]{2,1,0:T(8,128)S(1)}, u32[]{:S(2)}, u32[]{:S(2)}) collective-permute-start(f32[9,16,512]{2,1,0:T(8,128)S(1)} %get-tuple-element.20.z_high), channel_id=1, source_target_pairs={{0,1},{1,2},{2,3},{3,4},{4,5},{5,6},{6,7},{7,8},{8,9},{9,10},{10,1... | collective-permute-start | bytes 884744 | tf_op jit(solution)/shard_map/ppermute | solution.py:265

commit v2 on v1

v2 whole, which is shorter than its diff:
```python
import functools
import jax
import jax.numpy as jnp
from jax import lax
from jax.experimental import pallas as pl
from jax.experimental.pallas import tpu as pltpu
from jax.sharding import PartitionSpec as P

F32 = jnp.float32
BF16 = jnp.bfloat16


def harmonic(first_value, second_value):
    return 2.0 * first_value * second_value / (first_value + second_value)


def permit(classes, table):
    value = jnp.where(classes == 0, table[0], 0.0)
    for index in range(1, table.shape[0]):
        value = jnp.where(classes == index, table[index], value)
    return value


def split(rows):
    high = rows.astype(BF16)
    low = (rows - high.astype(F32)).astype(BF16)
    return jnp.concatenate([high, low], axis=0)


def products(left, right):
    return lax.dot_general(left, right, (((1,), (1,)), ((), ())), preferred_element_type=F32)


def fold(full, count, points):
    size = count * points
    total = (full[:size, :size] + full[:size, size:]) + (full[size:, :size] + full[size:, size:])
    row = lax.broadcasted_iota(jnp.int32, (size, size), 0)
    column = lax.broadcasted_iota(jnp.int32, (size, size), 1)
    total = jnp.where(lax.rem(row, points) == lax.rem(column, points), total, 0.0)
    return jnp.sum(total.reshape(count, points, size), axis=1)


def faces_kernel(table_in, vectors, classes, x_a, x_b, z_a, z_b, held, table, sems):
    count, cells_x, cells_z, length = vectors.shape
    half = cells_x // 2
    slab_odd = lax.rem(lax.axis_index("gx"), 2)
    tile_odd = lax.rem(lax.axis_index("yz"), 2)
    table_copy = pltpu.make_async_copy(table_in, table, sems.at[0])
    table_copy.start()
    layers, copies = [], []
    for odd in range(2):
        layer = [
            pltpu.make_async_copy(classes.at[:, (cells_z - 1) * side], held.at[index], sems.at[1 + index])
            for index, side in enumerate((1 - odd, odd))
        ]
        face = [
            pltpu.make_async_copy(
                vectors.at[:, (1 - side) * half : (2 - side) * half, (cells_z - 1) * side],
                out.at[0:count],
                sems.at[5 + index],
            )
            for index, (out, side) in enumerate(((z_a, 1 - odd), (z_b, odd)))
        ]

        @pl.when(tile_odd == odd)
        def _():
            for copy in layer + face:
                copy.start()

        if odd == 0:
            layers += layer
            copies += face
    for index, (out, side) in enumerate(((x_a, 1 - slab_odd), (x_b, slab_odd))):
        at = (cells_x - 1) * side
        layer = pltpu.make_async_copy(classes.at[at], held.at[2 + index], sems.at[3 + index])
        layer.start()
        layers.append(layer)
        face = pltpu.make_async_copy(vectors.at[:, at], out.at[0:count], sems.at[7 + index])
        face.start()
        copies.append(face)
    table_copy.wait()
    for index, out in enumerate((z_a, z_b, x_a, x_b)):
        layers[index].wait()
        out[count:] = permit(held[index], table).reshape(out.shape[0] - count, out.shape[1], length)
    for copy in copies:
        copy.wait()


def block_kernel(
    chunks, table_in, vectors, classes, applied, own, z_faces, x_sums, z_sums,
    held, kinds, face_x, result, total, table, sems,
):
    count, cells_x, cells_z, length = vectors.shape
    step = cells_x // chunks
    kind_copy = pltpu.make_async_copy(classes, kinds, sems.at[0])
    kind_copy.start()
    table_copy = pltpu.make_async_copy(table_in, table, sems.at[7 + 2 * chunks])
    table_copy.start()
    loads, stores = [], []
    for chunk in range(chunks):
        planes = pl.ds(chunk * step, step)
        load = pltpu.make_async_copy(vectors.at[:, planes], held.at[:, planes], sems.at[1 + chunk])
        load.start()
        loads.append(load)
        stores.append(
            pltpu.make_async_copy(result.at[:, planes], applied.at[:, planes], sems.at[1 + chunks + chunk])
        )
    face_x[0] = jnp.zeros((cells_z, length), F32)
    total[...] = jnp.zeros_like(total)
    row = lax.broadcasted_iota(jnp.int32, (cells_z, length), 0)
    column = lax.broadcasted_iota(jnp.int32, (cells_z, length), 1)
    kind_copy.wait()
    table_copy.wait()

    def plane(index):
        before = jnp.maximum(index - 1, 0)
        after = jnp.minimum(index + 1, cells_x - 1)
        value = permit(kinds[index], table)
        value_after = permit(kinds[after], table)
        low_x = face_x[index]
        high_x = jnp.where(index + 1 < cells_x, harmonic(value, value_after), 0.0)
        face_x[index + 1] = high_x
        value_z = pltpu.roll(value, cells_z - 1, 0)
        value_y = pltpu.roll(value, length - 1, 1)
        high_z = jnp.where(row < cells_z - 1, harmonic(value, value_z), 0.0)
        high_y = jnp.where(column < length - 1, harmonic(value, value_y), 0.0)
        for k in range(count):
            here = held[k, index]
            flux = low_x * (here - held[k, before]) + high_x * (here - held[k, after])
            flux_z = high_z * (here - pltpu.roll(here, cells_z - 1, 0))
            flux = flux + (flux_z - pltpu.roll(flux_z, 1, 0))
            flux_y = high_y * (here - pltpu.roll(here, length - 1, 1))
            flux = flux + (flux_y - pltpu.roll(flux_y, 1, 1))
            result[k, index] = flux

    def gram(index):
        left = split(held[:, index].reshape(count * cells_z, length))
        right = split(result[:, index].reshape(count * cells_z, length))
        return products(left, right)

    def follow(index, carry):
        total[...] += gram(index - 1)
        plane(index)
        return carry

    loads[0].wait()
    plane(0)
    for chunk in range(chunks):
        if chunk + 1 < chunks:
            loads[chunk + 1].wait()
        lax.fori_loop(max(1, chunk * step), (chunk + 1) * step, follow, 0)
        stores[chunk].start()
    sides = [
        pltpu.make_async_copy(result.at[:, 0], x_sums.at[0], sems.at[1 + 2 * chunks]),
        pltpu.make_async_copy(result.at[:, cells_x - 1], x_sums.at[1], sems.at[2 + 2 * chunks]),
        pltpu.make_async_copy(result.at[:, :, 0], z_sums.at[0], sems.at[3 + 2 * chunks]),
        pltpu.make_async_copy(result.at[:, :, cells_z - 1], z_sums.at[1], sems.at[4 + 2 * chunks]),
        pltpu.make_async_copy(held.at[:, :, 0], z_faces.at[0], sems.at[5 + 2 * chunks]),
        pltpu.make_async_copy(held.at[:, :, cells_z - 1], z_faces.at[1], sems.at[6 + 2 * chunks]),
    ]
    for copy in sides:
        copy.start()
    own[...] = fold(total[...] + gram(cells_x - 1), count, cells_z)
    for copy in sides + stores:
        copy.wait()


def outer_kernel(
    applied_in, own, z_faces, x_sums, z_sums, x_a, x_b, z_a, z_b, from_x_a, from_x_b, from_z_a, from_z_b,
    applied, blocks, x_new, z_new, z_flux, sems,
):
    count, cells_x, cells_z, length = applied.shape
    slots, _, width = blocks.shape
    half = cells_x // 2
    slab, tile = lax.axis_index("gx"), lax.axis_index("yz")
    slabs, tiles = lax.axis_size("gx"), lax.axis_size("yz")
    slab_odd, tile_odd = lax.rem(slab, 2), lax.rem(tile, 2)

    def rows(block):
        return block.reshape(-1, length)

    crosses_z = []
    for side, mine, other in ((1 - tile_odd, z_a, from_z_a), (tile_odd, z_b, from_z_b)):
        met = jnp.logical_and(tile + 2 * side - 1 >= 0, tile + 2 * side - 1 < tiles)
        weight = jnp.where(met, harmonic(rows(mine[count:]), rows(other[count:])), 0.0)
        flux = z_faces[side] * weight
        z_new[side] = z_sums[side] + flux
        z_flux[side] = flux.reshape(count, 2, half, length)
    z_stores = [
        pltpu.make_async_copy(z_new.at[0], applied.at[:, :, 0], sems.at[0]),
        pltpu.make_async_copy(z_new.at[1], applied.at[:, :, cells_z - 1], sems.at[1]),
    ]
    for copy in z_stores:
        copy.start()
    fluxes_x = []
    for side, mine, other in ((1 - slab_odd, x_a, from_x_a), (slab_odd, x_b, from_x_b)):
        met = jnp.logical_and(slab + 2 * side - 1 >= 0, slab + 2 * side - 1 < slabs)
        weight = jnp.where(met, harmonic(mine[count], other[count]), 0.0)
        flux = mine[0:count] * weight
        x_new[side] = x_sums[side] + flux
        fluxes_x.append(flux)
    for side, end in ((0, 0), (1, cells_x - 1)):
        part, at = divmod(end, half)
        x_new[side, :, 0:1, :] += z_flux[0, :, part, at : at + 1, :]
        x_new[side, :, cells_z - 1 : cells_z, :] += z_flux[1, :, part, at : at + 1, :]

    own_z = products(split(rows(z_flux[0])), split(rows(z_faces[0])))
    own_z += products(split(rows(z_flux[1])), split(rows(z_faces[1])))
    for side, other in ((1 - tile_odd, from_z_a), (tile_odd, from_z_b)):
        left = split(rows(z_flux[side, :, side]))
        crosses_z.append(fold(products(left, split(rows(other[0:count]))), count, half))
    for copy in z_stores:
        copy.wait()
    x_stores = [
        pltpu.make_async_copy(x_new.at[0], applied.at[:, 0], sems.at[2]),
        pltpu.make_async_copy(x_new.at[1], applied.at[:, cells_x - 1], sems.at[3]),
    ]
    for copy in x_stores:
        copy.start()
    own_x, crosses_x = 0.0, []
    for flux, mine, other in zip(fluxes_x, (x_a, x_b), (from_x_a, from_x_b)):
        left = split(rows(flux))
        own_x += products(left, split(rows(mine[0:count])))
        crosses_x.append(fold(products(left, split(rows(other[0:count]))), count, cells_z))

    def placing(points, column):
        entry = lax.broadcasted_iota(jnp.int32, (count * points, width), 0)
        at = lax.broadcasted_iota(jnp.int32, (count * points, width), 1)
        return (lax.div(entry, points) + column * count == at).astype(F32)

    scale = 1.0 / (cells_z * length)
    highest = lax.Precision.HIGHEST
    self_rows = own[...] + fold(own_x, count, cells_z)
    stacked = jnp.concatenate([self_rows, -crosses_x[0], -crosses_x[1]], axis=0)
    placed = jnp.dot(stacked, placing(cells_z, tile), precision=highest, preferred_element_type=F32) * scale
    placed_z = jnp.dot(
        jnp.concatenate([fold(own_z, count, cells_x), -crosses_z[0], -crosses_z[1]], axis=1),
        jnp.concatenate(
            [
                placing(cells_x, tile),
                placing(half, tile + 1 - 2 * tile_odd),
                placing(half, tile + 2 * tile_odd - 1),
            ],
            axis=0,
        ),
        precision=highest,
        preferred_element_type=F32,
    )
    blocks[...] = jnp.zeros_like(blocks)
    blocks[slab] = placed[0:count] + placed_z * scale
    blocks[slab + 1 - 2 * slab_odd] = placed[count : 2 * count]
    slot_b = slab + 2 * slab_odd - 1

    @pl.when(jnp.logical_and(slot_b >= 0, slot_b < slots))
    def _():
        blocks[slot_b] = placed[2 * count : 3 * count]

    for copy in x_stores:
        copy.wait()


def finish_kernel(count, tile, coarse):
    size = tile.shape[0]
    row = lax.broadcasted_iota(jnp.int32, (size, size), 0)
    column = lax.broadcasted_iota(jnp.int32, (size, size), 1)
    value = tile[...]
    other = jnp.where(lax.div(row, count) == lax.div(column, count), 0.0, value.T)
    coarse[...] = value + other


def shards(vectors, classes, permittivity):
    count, cells_x, cells_z, length = vectors.shape
    slabs, tiles = lax.axis_size("gx"), lax.axis_size("yz")
    hbm = pl.BlockSpec(memory_space=pltpu.HBM)
    anywhere = pl.BlockSpec(memory_space=pl.ANY)
    vmem = pl.BlockSpec(memory_space=pltpu.VMEM)
    shape = jax.ShapeDtypeStruct
    limit = 24 * 1024 * 1024
    params = pltpu.CompilerParams(vmem_limit_bytes=limit)
    vectors = pltpu.with_memory_space_constraint(vectors, pltpu.HBM)
    classes = pltpu.with_memory_space_constraint(classes, pltpu.HBM)
    permittivity = pltpu.with_memory_space_constraint(permittivity, pltpu.HBM)

    half = cells_x // 2
    own_eps_z = cells_x // half
    x_a, x_b, z_a, z_b = pl.pallas_call(
        faces_kernel,
        out_shape=(
            shape((count + 1, cells_z, length), F32),
            shape((count + 1, cells_z, length), F32),
            shape((count + own_eps_z, half, length), F32),
            shape((count + own_eps_z, half, length), F32),
        ),
        in_specs=[hbm, hbm, hbm],
        out_specs=(vmem,) * 4,
        scratch_shapes=[
            pltpu.VMEM((4, cells_z, length), jnp.int32),
            pltpu.SMEM(permittivity.shape, F32),
            pltpu.SemaphoreType.DMA((9,)),
        ],
        compiler_params=params,
        name="faces",
    )(permittivity, vectors, classes)

    near_x, near_z = [], []
    for slab in range(slabs):
        for tile in range(tiles):
            here = slab * tiles + tile
            mate = (slab + 1 ^ 1) - 1
            near_x.append((here, mate * tiles + tile if 0 <= mate < slabs else slab * tiles + (tile ^ 2)))
            mate = (tile + 1 ^ 1) - 1
            near_z.append((here, slab * tiles + mate if 0 <= mate < tiles else (slab ^ 1) * tiles + tile))
    both = ("gx", "yz")
    from_z_b = lax.ppermute(z_b, both, near_z)
    from_x_b = lax.ppermute(x_b, both, near_x)
    from_z_a = lax.ppermute(z_a, "yz", [(i, i ^ 1) for i in range(tiles)])
    from_x_a = lax.ppermute(x_a, "gx", [(i, i ^ 1) for i in range(slabs)])

    chunks = 4
    applied, own, z_faces, x_sums, z_sums = pl.pallas_call(
        functools.partial(block_kernel, chunks),
        out_shape=(
            pltpu.HBM(vectors.shape, F32),
            shape((count, count * cells_z), F32),
            shape((2, count, cells_x, length), F32),
            shape((2, count, cells_z, length), F32),
            shape((2, count, cells_x, length), F32),
        ),
        in_specs=[hbm, hbm, hbm],
        out_specs=(hbm, vmem, anywhere, anywhere, anywhere),
        scratch_shapes=[
            pltpu.VMEM(vectors.shape, F32),
            pltpu.VMEM(classes.shape, jnp.int32),
            pltpu.VMEM((cells_x + 1, cells_z, length), F32),
            pltpu.VMEM(vectors.shape, F32),
            pltpu.VMEM((2 * count * cells_z, 2 * count * cells_z), F32),
            pltpu.SMEM(permittivity.shape, F32),
            pltpu.SemaphoreType.DMA((8 + 2 * chunks,)),
        ],
        compiler_params=params,
        cost_estimate=pl.CostEstimate(flops=5_000_000_000, bytes_accessed=20_000_000, transcendentals=0),
        name="block",
    )(permittivity, vectors, classes)

    applied, blocks = pl.pallas_call(
        outer_kernel,
        out_shape=(pltpu.HBM(vectors.shape, F32), shape((tiles, count, count * slabs), F32)),
        in_specs=[hbm] + [vmem] * 12,
        out_specs=(hbm, vmem),
        scratch_shapes=[
            pltpu.VMEM((2, count, cells_z, length), F32),
            pltpu.VMEM((2, count, cells_x, length), F32),
            pltpu.VMEM((2, count, 2, half, length), F32),
            pltpu.SemaphoreType.DMA((4,)),
        ],
        input_output_aliases={0: 0},
        compiler_params=params,
        name="outer",
    )(
        applied, own, z_faces, x_sums, z_sums, x_a, x_b, z_a, z_b,
        from_x_a, from_x_b, from_z_a, from_z_b,
    )
    tile = lax.all_to_all(blocks, "yz", split_axis=0, concat_axis=0, tiled=True)
    tile = tile.reshape(tiles * count, count * slabs)
    coarse = pl.pallas_call(
        functools.partial(finish_kernel, count),
        out_shape=shape(tile.shape, F32),
        in_specs=[vmem],
        out_specs=vmem,
        compiler_params=params,
        name="finish",
    )(tile)
    return (applied, coarse)


def solution(mesh):
    return jax.shard_map(
        shards,
        mesh=mesh,
        in_specs=(P(None, "gx", "yz", None), P("gx", "yz", None), P()),
        out_specs=(P(None, "gx", "yz", None), P("gx", "yz")),
        check_vma=False,
    )
```

time: 44 us -> 36.9 us (0.84)
  starting transfers between devices: 12 us -> 4.33 us
  blocking collectives: 14.5 us -> 19.9 us
  Pallas kernels: 15.9 us -> 11.8 us
  local copies, waits for them, and re-layouts: 0.65 us -> 0 us
    ppermute x4, starting transfers between devices: 12 us -> 4.33 us  [the longest x1 2.43 us: shards(): from_x_b = lax.ppermute(x_b, both, near_x)]
    all_to_all x1, blocking collectives: 14.5 us -> 19.9 us  [shards(): tile = lax.all_to_all(blocks, 'yz', split_axis=0, concat_axis=0, tiled=True)]
    pallas_call x1, Pallas kernels: 11 us -> 7.61 us  [shards(): pl.pallas_call(functools.partial(block_kernel, chunks), out_shape=(pltpu....]
    unnamed x4 -> x0, local copies, waits for them, and re-layouts: 0.65 us -> none
    pallas_call x1, Pallas kernels: 1.86 us -> 1.37 us  [shards(): pl.pallas_call(faces_kernel, out_shape=(shape((count + 1, cells_z, length...]
  transfers between devices with their start and end apart: 4 -> 4, of which waited for: 0 -> 0; matrix products, arithmetic and copies ran while one was open for 0% -> 0% of each run, Pallas kernels for 25% -> 21%
where the time goes in v2:
time: 36.9 us; the launch traced here: 36.8 us
  blocking collectives  19.9 us (54%)
  Pallas kernels  11.8 us (32%)
  starting transfers between devices  4.33 us (12%)
  between operations  0.69 us (2%)
    all_to_all x1, blocking collectives, shards(): tile = lax.all_to_all(blocks, 'yz', split_axis=0, concat_axis=0, tiled=True)  19.9 us
    pallas_call x1, Pallas kernels, shards(): pl.pallas_call(functools.partial(block_kernel, chunks), out_shape=(pltpu....  7.61 us
    ppermute x1, starting transfers between devices, shards(): from_x_b = lax.ppermute(x_b, both, near_x)  2.43 us
    pallas_call x1, Pallas kernels, shards(): pl.pallas_call(outer_kernel, out_shape=(pltpu.HBM(vectors.shape, F32), sh...  2.09 us
    ppermute x1, starting transfers between devices, shards(): from_z_a = lax.ppermute(z_a, 'yz', [(i, i ^ 1) for i in range(tiles)])  1.39 us
    pallas_call x1, Pallas kernels, shards(): pl.pallas_call(faces_kernel, out_shape=(shape((count + 1, cells_z, length...  1.37 us
  transfers between devices with their start and end apart: 4, of which 0 were waited for; matrix products, arithmetic and copies ran while one was open for 0% of the time, Pallas kernels for 21%

profile of v2, /device:TPU:16, one launch (start us, length us, event | category | flops | bytes accessed | tf_op | source)
XLA Modules:
  0.0 36.8 jit_solution(13536474506991975214)
XLA Ops:
  0.6 1.4 %faces.1 = (f32[9,16,512]{2,1,0:T(8,128)S(1)}, f32[9,16,512]{2,1,0:T(8,128)S(1)}, f32[10,8,512]{2,1,0:T(8,128)S(1)}, f32[10,8,512]{2,1,0:T(8,128)S(1)}) custom-call(f32[4]{0:T(128)} %table_in.3, f32[8,16,16,512]{3,2,1,0:T(8,128)} %vectors.3, s32[16,16,512]{2,1,0:T(8,128)} %classes.3), custom_call_target="tpu_custom_call" | custom-call | tf_op jit(solution)/shard_map/faces/pallas_call | solution.py:286
  2.0 1.4 %collective-permute-start.2 = (f32[10,8,512]{2,1,0:T(8,128)S(1)}, f32[10,8,512]{2,1,0:T(8,128)S(1)}, u32[]{:S(2)}, u32[]{:S(2)}) collective-permute-start(f32[10,8,512]{2,1,0:T(8,128)S(1)} %get-tuple-element.20.z_a), channel_id=1, source_target_pairs={{0,1},{1,0},{2,3},{3,2},{4,5},{5,4},{6,7},{7,6},{8,9},{9,8},{10,11... | collective-permute-start | bytes 491528 | tf_op jit(solution)/shard_map/ppermute | solution.py:316
  3.4 0.0 collective-permute-start.3
  3.4 0.5 %collective-permute-start = (f32[9,16,512]{2,1,0:T(8,128)S(1)}, f32[9,16,512]{2,1,0:T(8,128)S(1)}, u32[]{:S(2)}, u32[]{:S(2)}) collective-permute-start(f32[9,16,512]{2,1,0:T(8,128)S(1)} %get-tuple-element.18.x_a), channel_id=1, source_target_pairs={{0,16},{16,0},{32,48},{48,32},{64,80},{80,64},{96,112},{112,96},{1... | collective-permute-start | bytes 884744 | tf_op jit(solution)/shard_map/ppermute | solution.py:317
  3.9 2.4 %collective-permute-start.1 = (f32[9,16,512]{2,1,0:T(8,128)S(1)}, f32[9,16,512]{2,1,0:T(8,128)S(1)}, u32[]{:S(2)}, u32[]{:S(2)}) collective-permute-start(f32[9,16,512]{2,1,0:T(8,128)S(1)} %get-tuple-element.19.x_b), channel_id=1, source_target_pairs={{0,2},{1,3},{2,0},{3,1},{4,6},{5,7},{6,4},{7,5},{8,10},{9,11},{10,... | collective-permute-start | bytes 884744 | tf_op jit(solution)/shard_map/ppermute | solution.py:315
  6.3 7.6 %block.1 = (f32[8,16,16,512]{3,2,1,0:T(8,128)}, f32[8,128]{1,0:T(8,128)S(1)}, f32[2,8,16,512]{3,2,1,0:T(8,128)S(1)}, f32[2,8,16,512]{3,2,1,0:T(8,128)S(1)}, f32[2,8,16,512]{3,2,1,0:T(8,128)S(1)}) custom-call(f32[4]{0:T(128)} %table_in.3, f32[8,16,16,512]{3,2,1,0:T(8,128)} %vectors.3, s32[16,16,512]{2,1,0:T(8,128)} %classes.3), custom_call_target="tpu_custom_call" | custom-call | flops 5000000000 | bytes 20000000 | tf_op jit(solution)/shard_map/block/pallas_call | solution.py:320
  14.0 0.0 collective-permute-done.2.from_z_a
  14.0 0.0 collective-permute-done.3.from_z_b
  14.0 0.0 collective-permute-done.from_x_a
  14.0 0.0 collective-permute-done.1.from_x_b
  14.0 2.1 %outer.1 = (f32[8,16,16,512]{3,2,1,0:T(8,128)}, f32[16,8,128]{2,1,0:T(8,128)S(1)}) custom-call(f32[8,16,16,512]{3,2,1,0:T(8,128)} %get-tuple-element.13.applied_in, f32[8,128]{1,0:T(8,128)S(1)} %get-tuple-element.14.own, f32[2,8,16,512]{3,2,1,0:T(8,128)S(1)} %get-tuple-element.15.z_faces, ...), custom_call_target="tpu_custom_call", output_to_operand_aliasing={{0}: (0, {})} | custom-call | tf_op jit(solution)/shard_map/outer/pallas_call | solution.py:345
  16.1 19.9 %all_to_all.5 = f32[16,8,128]{2,1,0:T(8,128)S(1)} all-to-all(f32[16,8,128]{2,1,0:T(8,128)S(1)} %get-tuple-element.23), channel_id=1, replica_groups=mesh['gx'=16,'yz'=16] {'yz'}, dimensions={0} | all-to-all | bytes 131072 | tf_op jit(solution)/shard_map/all_to_all | solution.py:363
  36.0 0.7 %finish.1 = f32[128,128]{1,0:T(8,128)} custom-call(f32[128,128]{1,0:T(8,128)S(1)} %bitcast.1), custom_call_target="tpu_custom_call" | custom-call | tf_op jit(solution)/shard_map/finish/pallas_call | solution.py:365
Async XLA Ops:
  2.0 12.0 %collective-permute-start.2 = (f32[10,8,512]{2,1,0:T(8,128)S(1)}, f32[10,8,512]{2,1,0:T(8,128)S(1)}, u32[]{:S(2)}, u32[]{:S(2)}) collective-permute-start(f32[10,8,512]{2,1,0:T(8,128)S(1)} %get-tuple-element.20.z_a), channel_id=1, source_target_pairs={{0,1},{1,0},{2,3},{3,2},{4,5},{5,4},{6,7},{7,6},{8,9},{9,8},{10,11... | collective-permute-start | bytes 491528 | tf_op jit(solution)/shard_map/ppermute | solution.py:316
  3.4 10.6 %collective-permute-start.3 = (f32[10,8,512]{2,1,0:T(8,128)S(1)}, f32[10,8,512]{2,1,0:T(8,128)S(1)}, u32[]{:S(2)}, u32[]{:S(2)}) collective-permute-start(f32[10,8,512]{2,1,0:T(8,128)S(1)} %get-tuple-element.21.z_b), channel_id=1, source_target_pairs={{0,16},{1,2},{2,1},{3,4},{4,3},{5,6},{6,5},{7,8},{8,7},{9,10},{10,... | collective-permute-start | bytes 491528 | tf_op jit(solution)/shard_map/ppermute | solution.py:314
  3.4 10.6 %collective-permute-start = (f32[9,16,512]{2,1,0:T(8,128)S(1)}, f32[9,16,512]{2,1,0:T(8,128)S(1)}, u32[]{:S(2)}, u32[]{:S(2)}) collective-permute-start(f32[9,16,512]{2,1,0:T(8,128)S(1)} %get-tuple-element.18.x_a), channel_id=1, source_target_pairs={{0,16},{16,0},{32,48},{48,32},{64,80},{80,64},{96,112},{112,96},{1... | collective-permute-start | bytes 884744 | tf_op jit(solution)/shard_map/ppermute | solution.py:317
  3.9 10.1 %collective-permute-start.1 = (f32[9,16,512]{2,1,0:T(8,128)S(1)}, f32[9,16,512]{2,1,0:T(8,128)S(1)}, u32[]{:S(2)}, u32[]{:S(2)}) collective-permute-start(f32[9,16,512]{2,1,0:T(8,128)S(1)} %get-tuple-element.19.x_b), channel_id=1, source_target_pairs={{0,2},{1,3},{2,0},{3,1},{4,6},{5,7},{6,4},{7,5},{8,10},{9,11},{10,... | collective-permute-start | bytes 884744 | tf_op jit(solution)/shard_map/ppermute | solution.py:315

commit v3 on v2

--- a/solution.py
+++ b/solution.py
@@ -36,8 +36,19 @@
     total = (full[:size, :size] + full[:size, size:]) + (full[size:, :size] + full[size:, size:])
     row = lax.broadcasted_iota(jnp.int32, (size, size), 0)
     column = lax.broadcasted_iota(jnp.int32, (size, size), 1)
-    total = jnp.where(lax.rem(row, points) == lax.rem(column, points), total, 0.0)
+    total = jnp.where(row & (points - 1) == column & (points - 1), total, 0.0)
     return jnp.sum(total.reshape(count, points, size), axis=1)
+
+
+def select(rows, places):
+    high = rows.astype(BF16)
+    rest = rows - high.astype(F32)
+    middle = rest.astype(BF16)
+    low = (rest - middle.astype(F32)).astype(BF16)
+    parts = jnp.concatenate([high, middle, low], axis=0)
+    summed = jnp.dot(parts, places.astype(BF16), preferred_element_type=F32)
+    size = rows.shape[0]
+    return (summed[2 * size :] + summed[size : 2 * size]) + summed[:size]
 
 
 def faces_kernel(table_in, vectors, classes, x_a, x_b, z_a, z_b, held, table, sems):
@@ -167,7 +178,7 @@
 
 def outer_kernel(
     applied_in, own, z_faces, x_sums, z_sums, x_a, x_b, z_a, z_b, from_x_a, from_x_b, from_z_a, from_z_b,
-    applied, blocks, x_new, z_new, z_flux, sems,
+    applied, x_new, blocks, z_new, z_flux, sems,
 ):
     count, cells_x, cells_z, length = applied.shape
     slots, _, width = blocks.shape
@@ -186,11 +197,11 @@
         flux = z_faces[side] * weight
         z_new[side] = z_sums[side] + flux
         z_flux[side] = flux.reshape(count, 2, half, length)
-    z_stores = [
+    stores = [
         pltpu.make_async_copy(z_new.at[0], applied.at[:, :, 0], sems.at[0]),
         pltpu.make_async_copy(z_new.at[1], applied.at[:, :, cells_z - 1], sems.at[1]),
     ]
-    for copy in z_stores:
+    for copy in stores:
         copy.start()
     fluxes_x = []
     for side, mine, other in ((1 - slab_odd, x_a, from_x_a), (slab_odd, x_b, from_x_b)):
@@ -203,69 +214,64 @@
         part, at = divmod(end, half)
         x_new[side, :, 0:1, :] += z_flux[0, :, part, at : at + 1, :]
         x_new[side, :, cells_z - 1 : cells_z, :] += z_flux[1, :, part, at : at + 1, :]
-
     own_z = products(split(rows(z_flux[0])), split(rows(z_faces[0])))
     own_z += products(split(rows(z_flux[1])), split(rows(z_faces[1])))
     for side, other in ((1 - tile_odd, from_z_a), (tile_odd, from_z_b)):
         left = split(rows(z_flux[side, :, side]))
         crosses_z.append(fold(products(left, split(rows(other[0:count]))), count, half))
-    for copy in z_stores:
-        copy.wait()
-    x_stores = [
-        pltpu.make_async_copy(x_new.at[0], applied.at[:, 0], sems.at[2]),
-        pltpu.make_async_copy(x_new.at[1], applied.at[:, cells_x - 1], sems.at[3]),
-    ]
-    for copy in x_stores:
-        copy.start()
     own_x, crosses_x = 0.0, []
     for flux, mine, other in zip(fluxes_x, (x_a, x_b), (from_x_a, from_x_b)):
         left = split(rows(flux))
         own_x += products(left, split(rows(mine[0:count])))
         crosses_x.append(fold(products(left, split(rows(other[0:count]))), count, cells_z))
 
-    def placing(points, column):
-        entry = lax.broadcasted_iota(jnp.int32, (count * points, width), 0)
-        at = lax.broadcasted_iota(jnp.int32, (count * points, width), 1)
-        return (lax.div(entry, points) + column * count == at).astype(F32)
-
     scale = 1.0 / (cells_z * length)
-    highest = lax.Precision.HIGHEST
-    self_rows = own[...] + fold(own_x, count, cells_z)
-    stacked = jnp.concatenate([self_rows, -crosses_x[0], -crosses_x[1]], axis=0)
-    placed = jnp.dot(stacked, placing(cells_z, tile), precision=highest, preferred_element_type=F32) * scale
-    placed_z = jnp.dot(
-        jnp.concatenate([fold(own_z, count, cells_x), -crosses_z[0], -crosses_z[1]], axis=1),
-        jnp.concatenate(
-            [
-                placing(cells_x, tile),
-                placing(half, tile + 1 - 2 * tile_odd),
-                placing(half, tile + 2 * tile_odd - 1),
-            ],
-            axis=0,
-        ),
-        precision=highest,
-        preferred_element_type=F32,
+    entry = lax.broadcasted_iota(jnp.int32, (width, width), 0)
+    column = lax.broadcasted_iota(jnp.int32, (width, width), 1)
+    place = (entry >> (cells_z.bit_length() - 1)) + tile * count == column
+    is_b = entry >= width // 2
+    tile_there = jnp.where(is_b, tile + 2 * tile_odd - 1, tile + 1 - 2 * tile_odd)
+    place_z = ((entry & (width // 2 - 1)) >> (half.bit_length() - 1)) + tile_there * count == column
+    stacked = jnp.concatenate(
+        [
+            own[...] + fold(own_x, count, cells_z) + fold(own_z, count, cells_x),
+            -crosses_x[0],
+            -crosses_x[1],
+            -jnp.concatenate(crosses_z, axis=1),
+        ],
+        axis=0,
     )
+    placed = select(stacked * scale, jnp.concatenate([place.astype(F32), place_z.astype(F32)], axis=1))
     blocks[...] = jnp.zeros_like(blocks)
-    blocks[slab] = placed[0:count] + placed_z * scale
-    blocks[slab + 1 - 2 * slab_odd] = placed[count : 2 * count]
+    blocks[slab] = placed[0:count, :width] + placed[3 * count :, width:]
+    blocks[slab + 1 - 2 * slab_odd] = placed[count : 2 * count, :width]
     slot_b = slab + 2 * slab_odd - 1
 
     @pl.when(jnp.logical_and(slot_b >= 0, slot_b < slots))
     def _():
-        blocks[slot_b] = placed[2 * count : 3 * count]
-
-    for copy in x_stores:
+        blocks[slot_b] = placed[2 * count : 3 * count, :width]
+
+    for copy in stores:
         copy.wait()
 
 
-def finish_kernel(count, tile, coarse):
+def finish_kernel(count, applied_in, x_new, tile, applied, coarse, summed, sems):
+    stores = [
+        pltpu.make_async_copy(x_new.at[0], applied.at[:, 0], sems.at[0]),
+        pltpu.make_async_copy(x_new.at[1], applied.at[:, applied.shape[1] - 1], sems.at[1]),
+    ]
+    for copy in stores:
+        copy.start()
     size = tile.shape[0]
     row = lax.broadcasted_iota(jnp.int32, (size, size), 0)
     column = lax.broadcasted_iota(jnp.int32, (size, size), 1)
+    shift = count.bit_length() - 1
     value = tile[...]
-    other = jnp.where(lax.div(row, count) == lax.div(column, count), 0.0, value.T)
-    coarse[...] = value + other
+    summed[...] = value + jnp.where(row >> shift == column >> shift, 0.0, value.T)
+    stores.append(pltpu.make_async_copy(summed, coarse, sems.at[2]))
+    stores[2].start()
+    for copy in stores:
+        copy.wait()
 
 
 def shards(vectors, classes, permittivity):
@@ -342,16 +348,19 @@
         name="block",
     )(permittivity, vectors, classes)
 
-    applied, blocks = pl.pallas_call(
+    applied, x_new, blocks = pl.pallas_call(
         outer_kernel,
-        out_shape=(pltpu.HBM(vectors.shape, F32), shape((tiles, count, count * slabs), F32)),
+        out_shape=(
+            pltpu.HBM(vectors.shape, F32),
+            shape((2, count, cells_z, length), F32),
+            shape((tiles, count, count * slabs), F32),
+        ),
         in_specs=[hbm] + [vmem] * 12,
-        out_specs=(hbm, vmem),
+        out_specs=(hbm, vmem, vmem),
         scratch_shapes=[
-            pltpu.VMEM((2, count, cells_z, length), F32),
             pltpu.VMEM((2, count, cells_x, length), F32),
             pltpu.VMEM((2, count, 2, half, length), F32),
-            pltpu.SemaphoreType.DMA((4,)),
+            pltpu.SemaphoreType.DMA((2,)),
         ],
         input_output_aliases={0: 0},
         compiler_params=params,
@@ -362,15 +371,16 @@
     )
     tile = lax.all_to_all(blocks, "yz", split_axis=0, concat_axis=0, tiled=True)
     tile = tile.reshape(tiles * count, count * slabs)
-    coarse = pl.pallas_call(
+    return pl.pallas_call(
         functools.partial(finish_kernel, count),
-        out_shape=shape(tile.shape, F32),
-        in_specs=[vmem],
-        out_specs=vmem,
+        out_shape=(pltpu.HBM(vectors.shape, F32), pltpu.HBM(tile.shape, F32)),
+        in_specs=[hbm, vmem, vmem],
+        out_specs=(hbm, hbm),
+        scratch_shapes=[pltpu.VMEM(tile.shape, F32), pltpu.SemaphoreType.DMA((3,))],
+        input_output_aliases={0: 0},
         compiler_params=params,
         name="finish",
-    )(tile)
-    return (applied, coarse)
+    )(applied, x_new, tile)
 
 
 def solution(mesh):

time: 36.9 us -> 36.2 us (0.981)
  Pallas kernels: 11.8 us -> 11.1 us
    pallas_call x1, Pallas kernels: 2.09 us -> 1.27 us  [shards(): pl.pallas_call(outer_kernel, out_shape=(pltpu.HBM(vectors.shape, F32), sh...]
where the time goes in v3:
time: 36.2 us; the launch traced here: 36.1 us
  blocking collectives  19.9 us (55%)
  Pallas kernels  11.1 us (31%)
  starting transfers between devices  4.33 us (12%)
  between operations  0.69 us (2%)
    all_to_all x1, blocking collectives, shards(): tile = lax.all_to_all(blocks, 'yz', split_axis=0, concat_axis=0, tiled=True)  19.9 us
    pallas_call x1, Pallas kernels, shards(): pl.pallas_call(functools.partial(block_kernel, chunks), out_shape=(pltpu....  7.61 us
    ppermute x1, starting transfers between devices, shards(): from_x_b = lax.ppermute(x_b, both, near_x)  2.43 us
    ppermute x1, starting transfers between devices, shards(): from_z_a = lax.ppermute(z_a, 'yz', [(i, i ^ 1) for i in range(tiles)])  1.39 us
    pallas_call x1, Pallas kernels, shards(): pl.pallas_call(faces_kernel, out_shape=(shape((count + 1, cells_z, length...  1.37 us
    pallas_call x1, Pallas kernels, shards(): pl.pallas_call(outer_kernel, out_shape=(pltpu.HBM(vectors.shape, F32), sh...  1.27 us
    pallas_call x1, Pallas kernels, shards(): pl.pallas_call(functools.partial(finish_kernel, count), out_shape=(pltpu....  0.83 us
  transfers between devices with their start and end apart: 4, of which 0 were waited for; matrix products, arithmetic and copies ran while one was open for 0% of the time, Pallas kernels for 21%

profile of v3, /device:TPU:16, one launch (start us, length us, event | category | flops | bytes accessed | tf_op | source)
XLA Modules:
  0.0 36.1 jit_solution(1776202952204201380)
XLA Ops:
  0.6 1.4 %faces.1 = (f32[9,16,512]{2,1,0:T(8,128)S(1)}, f32[9,16,512]{2,1,0:T(8,128)S(1)}, f32[10,8,512]{2,1,0:T(8,128)S(1)}, f32[10,8,512]{2,1,0:T(8,128)S(1)}) custom-call(f32[4]{0:T(128)} %table_in.3, f32[8,16,16,512]{3,2,1,0:T(8,128)} %vectors.3, s32[16,16,512]{2,1,0:T(8,128)} %classes.3), custom_call_target="tpu_custom_call" | custom-call | tf_op jit(solution)/shard_map/faces/pallas_call | solution.py:292
  2.0 1.4 %collective-permute-start.2 = (f32[10,8,512]{2,1,0:T(8,128)S(1)}, f32[10,8,512]{2,1,0:T(8,128)S(1)}, u32[]{:S(2)}, u32[]{:S(2)}) collective-permute-start(f32[10,8,512]{2,1,0:T(8,128)S(1)} %get-tuple-element.21.z_a), channel_id=1, source_target_pairs={{0,1},{1,0},{2,3},{3,2},{4,5},{5,4},{6,7},{7,6},{8,9},{9,8},{10,11... | collective-permute-start | bytes 491528 | tf_op jit(solution)/shard_map/ppermute | solution.py:322
  3.4 0.0 collective-permute-start.3
  3.4 0.5 %collective-permute-start = (f32[9,16,512]{2,1,0:T(8,128)S(1)}, f32[9,16,512]{2,1,0:T(8,128)S(1)}, u32[]{:S(2)}, u32[]{:S(2)}) collective-permute-start(f32[9,16,512]{2,1,0:T(8,128)S(1)} %get-tuple-element.19.x_a), channel_id=1, source_target_pairs={{0,16},{16,0},{32,48},{48,32},{64,80},{80,64},{96,112},{112,96},{1... | collective-permute-start | bytes 884744 | tf_op jit(solution)/shard_map/ppermute | solution.py:323
  3.9 2.4 %collective-permute-start.1 = (f32[9,16,512]{2,1,0:T(8,128)S(1)}, f32[9,16,512]{2,1,0:T(8,128)S(1)}, u32[]{:S(2)}, u32[]{:S(2)}) collective-permute-start(f32[9,16,512]{2,1,0:T(8,128)S(1)} %get-tuple-element.20.x_b), channel_id=1, source_target_pairs={{0,2},{1,3},{2,0},{3,1},{4,6},{5,7},{6,4},{7,5},{8,10},{9,11},{10,... | collective-permute-start | bytes 884744 | tf_op jit(solution)/shard_map/ppermute | solution.py:321
  6.3 7.6 %block.1 = (f32[8,16,16,512]{3,2,1,0:T(8,128)}, f32[8,128]{1,0:T(8,128)S(1)}, f32[2,8,16,512]{3,2,1,0:T(8,128)S(1)}, f32[2,8,16,512]{3,2,1,0:T(8,128)S(1)}, f32[2,8,16,512]{3,2,1,0:T(8,128)S(1)}) custom-call(f32[4]{0:T(128)} %table_in.3, f32[8,16,16,512]{3,2,1,0:T(8,128)} %vectors.3, s32[16,16,512]{2,1,0:T(8,128)} %classes.3), custom_call_target="tpu_custom_call" | custom-call | flops 5000000000 | bytes 20000000 | tf_op jit(solution)/shard_map/block/pallas_call | solution.py:326
  14.0 0.0 collective-permute-done.2.from_z_a
  14.0 0.0 collective-permute-done.3.from_z_b
  14.0 0.0 collective-permute-done.from_x_a
  14.0 0.0 collective-permute-done.1.from_x_b
  14.0 1.3 %outer.1 = (f32[8,16,16,512]{3,2,1,0:T(8,128)}, f32[2,8,16,512]{3,2,1,0:T(8,128)S(1)}, f32[16,8,128]{2,1,0:T(8,128)S(1)}) custom-call(f32[8,16,16,512]{3,2,1,0:T(8,128)} %get-tuple-element.14.applied_in, f32[8,128]{1,0:T(8,128)S(1)} %get-tuple-element.15.own, f32[2,8,16,512]{3,2,1,0:T(8,128)S(1)} %get-tuple-element.16.z_faces, ...), custom_call_target="tpu_custom_call", output_to_operand_aliasing={{0}: (0, {})} | custom-call | tf_op jit(solution)/shard_map/outer/pallas_call | solution.py:351
  15.3 19.9 %all_to_all.5 = f32[16,8,128]{2,1,0:T(8,128)S(1)} all-to-all(f32[16,8,128]{2,1,0:T(8,128)S(1)} %get-tuple-element.25), channel_id=1, replica_groups=mesh['gx'=16,'yz'=16] {'yz'}, dimensions={0} | all-to-all | bytes 131072 | tf_op jit(solution)/shard_map/all_to_all | solution.py:372
  35.2 0.8 %finish.1 = (f32[8,16,16,512]{3,2,1,0:T(8,128)}, f32[128,128]{1,0:T(8,128)}) custom-call(f32[8,16,16,512]{3,2,1,0:T(8,128)} %get-tuple-element.23.applied_in, f32[2,8,16,512]{3,2,1,0:T(8,128)S(1)} %get-tuple-element.24.x_new, f32[128,128]{1,0:T(8,128)S(1)} %bitcast.1), custom_call_target="tpu_custom_call", output_to_operand_aliasing={{0}: (0, {})} | custom-call | tf_op jit(solution)/shard_map/finish/pallas_call | solution.py:374
Async XLA Ops:
  2.0 12.0 %collective-permute-start.2 = (f32[10,8,512]{2,1,0:T(8,128)S(1)}, f32[10,8,512]{2,1,0:T(8,128)S(1)}, u32[]{:S(2)}, u32[]{:S(2)}) collective-permute-start(f32[10,8,512]{2,1,0:T(8,128)S(1)} %get-tuple-element.21.z_a), channel_id=1, source_target_pairs={{0,1},{1,0},{2,3},{3,2},{4,5},{5,4},{6,7},{7,6},{8,9},{9,8},{10,11... | collective-permute-start | bytes 491528 | tf_op jit(solution)/shard_map/ppermute | solution.py:322
  3.4 10.6 %collective-permute-start.3 = (f32[10,8,512]{2,1,0:T(8,128)S(1)}, f32[10,8,512]{2,1,0:T(8,128)S(1)}, u32[]{:S(2)}, u32[]{:S(2)}) collective-permute-start(f32[10,8,512]{2,1,0:T(8,128)S(1)} %get-tuple-element.22.z_b), channel_id=1, source_target_pairs={{0,16},{1,2},{2,1},{3,4},{4,3},{5,6},{6,5},{7,8},{8,7},{9,10},{10,... | collective-permute-start | bytes 491528 | tf_op jit(solution)/shard_map/ppermute | solution.py:320
  3.4 10.6 %collective-permute-start = (f32[9,16,512]{2,1,0:T(8,128)S(1)}, f32[9,16,512]{2,1,0:T(8,128)S(1)}, u32[]{:S(2)}, u32[]{:S(2)}) collective-permute-start(f32[9,16,512]{2,1,0:T(8,128)S(1)} %get-tuple-element.19.x_a), channel_id=1, source_target_pairs={{0,16},{16,0},{32,48},{48,32},{64,80},{80,64},{96,112},{112,96},{1... | collective-permute-start | bytes 884744 | tf_op jit(solution)/shard_map/ppermute | solution.py:323
  3.9 10.1 %collective-permute-start.1 = (f32[9,16,512]{2,1,0:T(8,128)S(1)}, f32[9,16,512]{2,1,0:T(8,128)S(1)}, u32[]{:S(2)}, u32[]{:S(2)}) collective-permute-start(f32[9,16,512]{2,1,0:T(8,128)S(1)} %get-tuple-element.20.x_b), channel_id=1, source_target_pairs={{0,2},{1,3},{2,0},{3,1},{4,6},{5,7},{6,4},{7,5},{8,10},{9,11},{10,... | collective-permute-start | bytes 884744 | tf_op jit(solution)/shard_map/ppermute | solution.py:321

commit v4 on v3

--- a/solution.py
+++ b/solution.py
@@ -16,7 +16,7 @@
 
 def permit(classes, table):
     value = jnp.where(classes == 0, table[0], 0.0)
-    for index in range(1, table.shape[0]):
+    for index in range(1, len(table)):
         value = jnp.where(classes == index, table[index], value)
     return value
 
@@ -51,12 +51,12 @@
     return (summed[2 * size :] + summed[size : 2 * size]) + summed[:size]
 
 
-def faces_kernel(table_in, vectors, classes, x_a, x_b, z_a, z_b, held, table, sems):
+def faces_kernel(table_in, vectors, classes, x_a, x_b, z_a, z_b, levels, held, table_ref, sems):
     count, cells_x, cells_z, length = vectors.shape
     half = cells_x // 2
     slab_odd = lax.rem(lax.axis_index("gx"), 2)
     tile_odd = lax.rem(lax.axis_index("yz"), 2)
-    table_copy = pltpu.make_async_copy(table_in, table, sems.at[0])
+    table_copy = pltpu.make_async_copy(table_in, table_ref, sems.at[0])
     table_copy.start()
     layers, copies = [], []
     for odd in range(2):
@@ -90,6 +90,9 @@
         face.start()
         copies.append(face)
     table_copy.wait()
+    table = [table_ref[index] for index in range(levels.shape[0])]
+    row = lax.broadcasted_iota(jnp.int32, levels.shape, 0)
+    levels[...] = permit(row, table)
     for index, out in enumerate((z_a, z_b, x_a, x_b)):
         layers[index].wait()
         out[count:] = permit(held[index], table).reshape(out.shape[0] - count, out.shape[1], length)
@@ -98,43 +101,42 @@
 
 
 def block_kernel(
-    chunks, table_in, vectors, classes, applied, own, z_faces, x_sums, z_sums,
-    held, kinds, face_x, result, total, table, sems,
+    chunks, levels, kinds, vectors, applied, own, z_faces, x_sums, z_sums,
+    held, face_x, face_z, face_y, result, total, sems,
 ):
     count, cells_x, cells_z, length = vectors.shape
     step = cells_x // chunks
-    kind_copy = pltpu.make_async_copy(classes, kinds, sems.at[0])
-    kind_copy.start()
-    table_copy = pltpu.make_async_copy(table_in, table, sems.at[7 + 2 * chunks])
-    table_copy.start()
     loads, stores = [], []
     for chunk in range(chunks):
         planes = pl.ds(chunk * step, step)
-        load = pltpu.make_async_copy(vectors.at[:, planes], held.at[:, planes], sems.at[1 + chunk])
+        load = pltpu.make_async_copy(vectors.at[:, planes], held.at[:, planes], sems.at[chunk])
         load.start()
         loads.append(load)
         stores.append(
-            pltpu.make_async_copy(result.at[:, planes], applied.at[:, planes], sems.at[1 + chunks + chunk])
+            pltpu.make_async_copy(result.at[:, planes], applied.at[:, planes], sems.at[chunks + chunk])
         )
-    face_x[0] = jnp.zeros((cells_z, length), F32)
     total[...] = jnp.zeros_like(total)
     row = lax.broadcasted_iota(jnp.int32, (cells_z, length), 0)
     column = lax.broadcasted_iota(jnp.int32, (cells_z, length), 1)
-    kind_copy.wait()
-    table_copy.wait()
+    table = [levels[index : index + 1, :] for index in range(levels.shape[0])]
+    face_x[0] = jnp.zeros((cells_z, length), F32)
+
+    def weigh(index, value):
+        value_after = permit(kinds[jnp.minimum(index + 1, cells_x - 1)], table)
+        face_x[index + 1] = jnp.where(index + 1 < cells_x, harmonic(value, value_after), 0.0)
+        value_z = pltpu.roll(value, cells_z - 1, 0)
+        value_y = pltpu.roll(value, length - 1, 1)
+        face_z[index] = jnp.where(row < cells_z - 1, harmonic(value, value_z), 0.0)
+        face_y[index] = jnp.where(column < length - 1, harmonic(value, value_y), 0.0)
+        return value_after
+
+    lax.fori_loop(0, cells_x, weigh, permit(kinds[0], table))
 
     def plane(index):
         before = jnp.maximum(index - 1, 0)
         after = jnp.minimum(index + 1, cells_x - 1)
-        value = permit(kinds[index], table)
-        value_after = permit(kinds[after], table)
-        low_x = face_x[index]
-        high_x = jnp.where(index + 1 < cells_x, harmonic(value, value_after), 0.0)
-        face_x[index + 1] = high_x
-        value_z = pltpu.roll(value, cells_z - 1, 0)
-        value_y = pltpu.roll(value, length - 1, 1)
-        high_z = jnp.where(row < cells_z - 1, harmonic(value, value_z), 0.0)
-        high_y = jnp.where(column < length - 1, harmonic(value, value_y), 0.0)
+        low_x, high_x = face_x[index], face_x[index + 1]
+        high_z, high_y = face_z[index], face_y[index]
         for k in range(count):
             here = held[k, index]
             flux = low_x * (here - held[k, before]) + high_x * (here - held[k, after])
@@ -162,12 +164,12 @@
         lax.fori_loop(max(1, chunk * step), (chunk + 1) * step, follow, 0)
         stores[chunk].start()
     sides = [
-        pltpu.make_async_copy(result.at[:, 0], x_sums.at[0], sems.at[1 + 2 * chunks]),
-        pltpu.make_async_copy(result.at[:, cells_x - 1], x_sums.at[1], sems.at[2 + 2 * chunks]),
-        pltpu.make_async_copy(result.at[:, :, 0], z_sums.at[0], sems.at[3 + 2 * chunks]),
-        pltpu.make_async_copy(result.at[:, :, cells_z - 1], z_sums.at[1], sems.at[4 + 2 * chunks]),
-        pltpu.make_async_copy(held.at[:, :, 0], z_faces.at[0], sems.at[5 + 2 * chunks]),
-        pltpu.make_async_copy(held.at[:, :, cells_z - 1], z_faces.at[1], sems.at[6 + 2 * chunks]),
+        pltpu.make_async_copy(result.at[:, 0], x_sums.at[0], sems.at[2 * chunks]),
+        pltpu.make_async_copy(result.at[:, cells_x - 1], x_sums.at[1], sems.at[1 + 2 * chunks]),
+        pltpu.make_async_copy(result.at[:, :, 0], z_sums.at[0], sems.at[2 + 2 * chunks]),
+        pltpu.make_async_copy(result.at[:, :, cells_z - 1], z_sums.at[1], sems.at[3 + 2 * chunks]),
+        pltpu.make_async_copy(held.at[:, :, 0], z_faces.at[0], sems.at[4 + 2 * chunks]),
+        pltpu.make_async_copy(held.at[:, :, cells_z - 1], z_faces.at[1], sems.at[5 + 2 * chunks]),
     ]
     for copy in sides:
         copy.start()
@@ -283,22 +285,24 @@
     shape = jax.ShapeDtypeStruct
     limit = 24 * 1024 * 1024
     params = pltpu.CompilerParams(vmem_limit_bytes=limit)
+    classes_in = classes
     vectors = pltpu.with_memory_space_constraint(vectors, pltpu.HBM)
     classes = pltpu.with_memory_space_constraint(classes, pltpu.HBM)
     permittivity = pltpu.with_memory_space_constraint(permittivity, pltpu.HBM)
 
     half = cells_x // 2
     own_eps_z = cells_x // half
-    x_a, x_b, z_a, z_b = pl.pallas_call(
+    x_a, x_b, z_a, z_b, levels = pl.pallas_call(
         faces_kernel,
         out_shape=(
             shape((count + 1, cells_z, length), F32),
             shape((count + 1, cells_z, length), F32),
             shape((count + own_eps_z, half, length), F32),
             shape((count + own_eps_z, half, length), F32),
+            shape((permittivity.shape[0], length), F32),
         ),
         in_specs=[hbm, hbm, hbm],
-        out_specs=(vmem,) * 4,
+        out_specs=(vmem,) * 5,
         scratch_shapes=[
             pltpu.VMEM((4, cells_z, length), jnp.int32),
             pltpu.SMEM(permittivity.shape, F32),
@@ -332,21 +336,21 @@
             shape((2, count, cells_z, length), F32),
             shape((2, count, cells_x, length), F32),
         ),
-        in_specs=[hbm, hbm, hbm],
+        in_specs=[vmem, vmem, hbm],
         out_specs=(hbm, vmem, anywhere, anywhere, anywhere),
         scratch_shapes=[
             pltpu.VMEM(vectors.shape, F32),
-            pltpu.VMEM(classes.shape, jnp.int32),
             pltpu.VMEM((cells_x + 1, cells_z, length), F32),
+            pltpu.VMEM(classes.shape, F32),
+            pltpu.VMEM(classes.shape, F32),
             pltpu.VMEM(vectors.shape, F32),
             pltpu.VMEM((2 * count * cells_z, 2 * count * cells_z), F32),
-            pltpu.SMEM(permittivity.shape, F32),
-            pltpu.SemaphoreType.DMA((8 + 2 * chunks,)),
+            pltpu.SemaphoreType.DMA((6 + 2 * chunks,)),
         ],
         compiler_params=params,
         cost_estimate=pl.CostEstimate(flops=5_000_000_000, bytes_accessed=20_000_000, transcendentals=0),
         name="block",
-    )(permittivity, vectors, classes)
+    )(levels, classes_in, vectors)
 
     applied, x_new, blocks = pl.pallas_call(
         outer_kernel,

time: 36.2 us -> 35.9 us (level)
  transfers between devices with their start and end apart: 4 -> 4, of which waited for: 0 -> 1; matrix products, arithmetic and copies ran while one was open for 0% -> 0% of each run, Pallas kernels for 21% -> 20%
where the time goes in v4:
time: 35.9 us; the launch traced here: 35.7 us
  blocking collectives  19.9 us (55%)
  Pallas kernels  10.8 us (30%)
  starting transfers between devices  4.33 us (12%)
  between operations  0.69 us (2%)
    all_to_all x1, blocking collectives, shards(): tile = lax.all_to_all(blocks, 'yz', split_axis=0, concat_axis=0, tiled=True)  19.9 us
    pallas_call x1, Pallas kernels, shards(): pl.pallas_call(functools.partial(block_kernel, chunks), out_shape=(pltpu....  7.26 us
    ppermute x1, starting transfers between devices, shards(): from_x_b = lax.ppermute(x_b, both, near_x)  2.43 us
    pallas_call x1, Pallas kernels, shards(): pl.pallas_call(faces_kernel, out_shape=(shape((count + 1, cells_z, length...  1.42 us
    ppermute x1, starting transfers between devices, shards(): from_z_a = lax.ppermute(z_a, 'yz', [(i, i ^ 1) for i in range(tiles)])  1.39 us
    pallas_call x1, Pallas kernels, shards(): pl.pallas_call(outer_kernel, out_shape=(pltpu.HBM(vectors.shape, F32), sh...  1.24 us
    pallas_call x1, Pallas kernels, shards(): pl.pallas_call(functools.partial(finish_kernel, count), out_shape=(pltpu....  0.83 us
  transfers between devices with their start and end apart: 4, of which 1 were waited for; matrix products, arithmetic and copies ran while one was open for 0% of the time, Pallas kernels for 20%

profile of v4, /device:TPU:16, one launch (start us, length us, event | category | flops | bytes accessed | tf_op | source)
XLA Modules:
  0.0 35.7 jit_solution(13681466551936508039)
XLA Ops:
  0.6 0.0 copy-start
  0.6 1.4 %faces.1 = (f32[9,16,512]{2,1,0:T(8,128)S(1)}, f32[9,16,512]{2,1,0:T(8,128)S(1)}, f32[10,8,512]{2,1,0:T(8,128)S(1)}, f32[10,8,512]{2,1,0:T(8,128)S(1)}, f32[4,512]{1,0:T(4,128)S(1)}) custom-call(f32[4]{0:T(128)} %table_in.1, f32[8,16,16,512]{3,2,1,0:T(8,128)} %vectors.3, s32[16,16,512]{2,1,0:T(8,128)} %kinds.1), custom_call_target="tpu_custom_call" | custom-call | tf_op jit(solution)/shard_map/faces/pallas_call | solution.py:295
  2.1 1.4 %collective-permute-start.2 = (f32[10,8,512]{2,1,0:T(8,128)S(1)}, f32[10,8,512]{2,1,0:T(8,128)S(1)}, u32[]{:S(2)}, u32[]{:S(2)}) collective-permute-start(f32[10,8,512]{2,1,0:T(8,128)S(1)} %get-tuple-element.23.z_a), channel_id=1, source_target_pairs={{0,1},{1,0},{2,3},{3,2},{4,5},{5,4},{6,7},{7,6},{8,9},{9,8},{10,11... | collective-permute-start | bytes 491528 | tf_op jit(solution)/shard_map/ppermute | solution.py:326
  3.5 0.0 collective-permute-start.3
  3.5 0.5 %collective-permute-start = (f32[9,16,512]{2,1,0:T(8,128)S(1)}, f32[9,16,512]{2,1,0:T(8,128)S(1)}, u32[]{:S(2)}, u32[]{:S(2)}) collective-permute-start(f32[9,16,512]{2,1,0:T(8,128)S(1)} %get-tuple-element.21.x_a), channel_id=1, source_target_pairs={{0,16},{16,0},{32,48},{48,32},{64,80},{80,64},{96,112},{112,96},{1... | collective-permute-start | bytes 884744 | tf_op jit(solution)/shard_map/ppermute | solution.py:327
  4.0 2.4 %collective-permute-start.1 = (f32[9,16,512]{2,1,0:T(8,128)S(1)}, f32[9,16,512]{2,1,0:T(8,128)S(1)}, u32[]{:S(2)}, u32[]{:S(2)}) collective-permute-start(f32[9,16,512]{2,1,0:T(8,128)S(1)} %get-tuple-element.22.x_b), channel_id=1, source_target_pairs={{0,2},{1,3},{2,0},{3,1},{4,6},{5,7},{6,4},{7,5},{8,10},{9,11},{10,... | collective-permute-start | bytes 884744 | tf_op jit(solution)/shard_map/ppermute | solution.py:325
  6.4 0.0 copy-done
  6.4 7.3 %block.1 = (f32[8,16,16,512]{3,2,1,0:T(8,128)}, f32[8,128]{1,0:T(8,128)S(1)}, f32[2,8,16,512]{3,2,1,0:T(8,128)S(1)}, f32[2,8,16,512]{3,2,1,0:T(8,128)S(1)}, f32[2,8,16,512]{3,2,1,0:T(8,128)S(1)}) custom-call(f32[4,512]{1,0:T(4,128)S(1)} %get-tuple-element.15.levels, s32[16,16,512]{2,1,0:T(8,128)S(1)} %copy-done, f32[8,16,16,512]{3,2,1,0:T(8,128)} %vectors.3), custom_call_target="tpu_custom_call" | custom-call | flops 5000000000 | bytes 20000000 | tf_op jit(solution)/shard_map/block/pallas_call | solution.py:330
  13.7 0.0 collective-permute-done.2.from_z_a
  13.7 0.0 collective-permute-done.3.from_z_b
  13.7 0.0 collective-permute-done.from_x_a
  13.7 0.1 collective-permute-done.1.from_x_b
  13.8 1.2 %outer.1 = (f32[8,16,16,512]{3,2,1,0:T(8,128)}, f32[2,8,16,512]{3,2,1,0:T(8,128)S(1)}, f32[16,8,128]{2,1,0:T(8,128)S(1)}) custom-call(f32[8,16,16,512]{3,2,1,0:T(8,128)} %get-tuple-element.16.applied_in, f32[8,128]{1,0:T(8,128)S(1)} %get-tuple-element.17.own, f32[2,8,16,512]{3,2,1,0:T(8,128)S(1)} %get-tuple-element.18.z_faces, ...), custom_call_target="tpu_custom_call", output_to_operand_aliasing={{0}: (0, {})} | custom-call | tf_op jit(solution)/shard_map/outer/pallas_call | solution.py:355
  15.0 19.9 %all_to_all.5 = f32[16,8,128]{2,1,0:T(8,128)S(1)} all-to-all(f32[16,8,128]{2,1,0:T(8,128)S(1)} %get-tuple-element.27), channel_id=1, replica_groups=mesh['gx'=16,'yz'=16] {'yz'}, dimensions={0} | all-to-all | bytes 131072 | tf_op jit(solution)/shard_map/all_to_all | solution.py:376
  34.9 0.8 %finish.1 = (f32[8,16,16,512]{3,2,1,0:T(8,128)}, f32[128,128]{1,0:T(8,128)}) custom-call(f32[8,16,16,512]{3,2,1,0:T(8,128)} %get-tuple-element.25.applied_in, f32[2,8,16,512]{3,2,1,0:T(8,128)S(1)} %get-tuple-element.26.x_new, f32[128,128]{1,0:T(8,128)S(1)} %bitcast.1), custom_call_target="tpu_custom_call", output_to_operand_aliasing={{0}: (0, {})} | custom-call | tf_op jit(solution)/shard_map/finish/pallas_call | solution.py:378
Async XLA Ops:
  0.6 5.8 %copy-start = (s32[16,16,512]{2,1,0:T(8,128)S(1)}, s32[16,16,512]{2,1,0:T(8,128)}, u32[]{:S(2)}) copy-start(s32[16,16,512]{2,1,0:T(8,128)} %kinds.1) | copy-start | bytes 1572868
  2.1 11.6 %collective-permute-start.2 = (f32[10,8,512]{2,1,0:T(8,128)S(1)}, f32[10,8,512]{2,1,0:T(8,128)S(1)}, u32[]{:S(2)}, u32[]{:S(2)}) collective-permute-start(f32[10,8,512]{2,1,0:T(8,128)S(1)} %get-tuple-element.23.z_a), channel_id=1, source_target_pairs={{0,1},{1,0},{2,3},{3,2},{4,5},{5,4},{6,7},{7,6},{8,9},{9,8},{10,11... | collective-permute-start | bytes 491528 | tf_op jit(solution)/shard_map/ppermute | solution.py:326
  3.5 10.2 %collective-permute-start.3 = (f32[10,8,512]{2,1,0:T(8,128)S(1)}, f32[10,8,512]{2,1,0:T(8,128)S(1)}, u32[]{:S(2)}, u32[]{:S(2)}) collective-permute-start(f32[10,8,512]{2,1,0:T(8,128)S(1)} %get-tuple-element.24.z_b), channel_id=1, source_target_pairs={{0,16},{1,2},{2,1},{3,4},{4,3},{5,6},{6,5},{7,8},{8,7},{9,10},{10,... | collective-permute-start | bytes 491528 | tf_op jit(solution)/shard_map/ppermute | solution.py:324
  3.5 10.2 %collective-permute-start = (f32[9,16,512]{2,1,0:T(8,128)S(1)}, f32[9,16,512]{2,1,0:T(8,128)S(1)}, u32[]{:S(2)}, u32[]{:S(2)}) collective-permute-start(f32[9,16,512]{2,1,0:T(8,128)S(1)} %get-tuple-element.21.x_a), channel_id=1, source_target_pairs={{0,16},{16,0},{32,48},{48,32},{64,80},{80,64},{96,112},{112,96},{1... | collective-permute-start | bytes 884744 | tf_op jit(solution)/shard_map/ppermute | solution.py:327
  4.0 9.8 %collective-permute-start.1 = (f32[9,16,512]{2,1,0:T(8,128)S(1)}, f32[9,16,512]{2,1,0:T(8,128)S(1)}, u32[]{:S(2)}, u32[]{:S(2)}) collective-permute-start(f32[9,16,512]{2,1,0:T(8,128)S(1)} %get-tuple-element.22.x_b), channel_id=1, source_target_pairs={{0,2},{1,3},{2,0},{3,1},{4,6},{5,7},{6,4},{7,5},{8,10},{9,11},{10,... | collective-permute-start | bytes 884744 | tf_op jit(solution)/shard_map/ppermute | solution.py:325

commit v5 on v4

--- a/solution.py
+++ b/solution.py
@@ -179,7 +179,7 @@
 
 
 def outer_kernel(
-    applied_in, own, z_faces, x_sums, z_sums, x_a, x_b, z_a, z_b, from_x_a, from_x_b, from_z_a, from_z_b,
+    applied_in, own, z_faces, x_sums, z_sums, z_a, z_b, x_b, x_a, from_x_a, from_x_b, from_z_a, from_z_b,
     applied, x_new, blocks, z_new, z_flux, sems,
 ):
     count, cells_x, cells_z, length = applied.shape
@@ -370,7 +370,7 @@
         compiler_params=params,
         name="outer",
     )(
-        applied, own, z_faces, x_sums, z_sums, x_a, x_b, z_a, z_b,
+        applied, own, z_faces, x_sums, z_sums, z_a, z_b, x_b, x_a,
         from_x_a, from_x_b, from_z_a, from_z_b,
     )
     tile = lax.all_to_all(blocks, "yz", split_axis=0, concat_axis=0, tiled=True)

time: 35.9 us -> 35.4 us (0.986)
  the two profiles are of different devices: /device:TPU:16 before, /device:TPU:6 now
where the time goes in v5:
time: 35.4 us; the launch traced here: 35.3 us
  blocking collectives  19.2 us (54%)
  Pallas kernels  10.8 us (31%)
  starting transfers between devices  4.61 us (13%)
  between operations  0.7 us (2%)
    all_to_all x1, blocking collectives, shards(): tile = lax.all_to_all(blocks, 'yz', split_axis=0, concat_axis=0, tiled=True)  19.2 us
    pallas_call x1, Pallas kernels, shards(): pl.pallas_call(functools.partial(block_kernel, chunks), out_shape=(pltpu....  7.26 us
    ppermute x1, starting transfers between devices, shards(): from_x_a = lax.ppermute(x_a, 'gx', [(i, i ^ 1) for i in range(slabs)])  1.99 us
    ppermute x1, starting transfers between devices, shards(): from_z_a = lax.ppermute(z_a, 'yz', [(i, i ^ 1) for i in range(tiles)])  1.68 us
    pallas_call x1, Pallas kernels, shards(): pl.pallas_call(faces_kernel, out_shape=(shape((count + 1, cells_z, length...  1.42 us
    pallas_call x1, Pallas kernels, shards(): pl.pallas_call(outer_kernel, out_shape=(pltpu.HBM(vectors.shape, F32), sh...  1.25 us
    ppermute x1, starting transfers between devices, shards(): from_x_b = lax.ppermute(x_b, both, near_x)  0.94 us
    pallas_call x1, Pallas kernels, shards(): pl.pallas_call(functools.partial(finish_kernel, count), out_shape=(pltpu....  0.83 us
  transfers between devices with their start and end apart: 4, of which 0 were waited for; matrix products, arithmetic and copies ran while one was open for 0% of the time, Pallas kernels for 21%

profile of v5, /device:TPU:6, one launch (start us, length us, event | category | flops | bytes accessed | tf_op | source)
XLA Modules:
  0.0 35.3 jit_solution(17649766122647001287)
XLA Ops:
  0.6 0.0 copy-start
  0.6 1.4 %faces.1 = (f32[9,16,512]{2,1,0:T(8,128)S(1)}, f32[9,16,512]{2,1,0:T(8,128)S(1)}, f32[10,8,512]{2,1,0:T(8,128)S(1)}, f32[10,8,512]{2,1,0:T(8,128)S(1)}, f32[4,512]{1,0:T(4,128)S(1)}) custom-call(f32[4]{0:T(128)} %table_in.1, f32[8,16,16,512]{3,2,1,0:T(8,128)} %vectors.3, s32[16,16,512]{2,1,0:T(8,128)} %kinds.1), custom_call_target="tpu_custom_call" | custom-call | tf_op jit(solution)/shard_map/faces/pallas_call | solution.py:295
  2.1 1.7 %collective-permute-start.2 = (f32[10,8,512]{2,1,0:T(8,128)S(1)}, f32[10,8,512]{2,1,0:T(8,128)S(1)}, u32[]{:S(2)}, u32[]{:S(2)}) collective-permute-start(f32[10,8,512]{2,1,0:T(8,128)S(1)} %get-tuple-element.21.z_a), channel_id=1, source_target_pairs={{0,1},{1,0},{2,3},{3,2},{4,5},{5,4},{6,7},{7,6},{8,9},{9,8},{10,11... | collective-permute-start | bytes 491528 | tf_op jit(solution)/shard_map/ppermute | solution.py:326
  3.7 0.0 collective-permute-start.3
  3.8 0.9 %collective-permute-start.1 = (f32[9,16,512]{2,1,0:T(8,128)S(1)}, f32[9,16,512]{2,1,0:T(8,128)S(1)}, u32[]{:S(2)}, u32[]{:S(2)}) collective-permute-start(f32[9,16,512]{2,1,0:T(8,128)S(1)} %get-tuple-element.23.x_b), channel_id=1, source_target_pairs={{0,2},{1,3},{2,0},{3,1},{4,6},{5,7},{6,4},{7,5},{8,10},{9,11},{10,... | collective-permute-start | bytes 884744 | tf_op jit(solution)/shard_map/ppermute | solution.py:325
  4.7 2.0 %collective-permute-start = (f32[9,16,512]{2,1,0:T(8,128)S(1)}, f32[9,16,512]{2,1,0:T(8,128)S(1)}, u32[]{:S(2)}, u32[]{:S(2)}) collective-permute-start(f32[9,16,512]{2,1,0:T(8,128)S(1)} %get-tuple-element.24.x_a), channel_id=1, source_target_pairs={{0,16},{16,0},{32,48},{48,32},{64,80},{80,64},{96,112},{112,96},{1... | collective-permute-start | bytes 884744 | tf_op jit(solution)/shard_map/ppermute | solution.py:327
  6.7 0.0 copy-done
  6.7 7.3 %block.1 = (f32[8,16,16,512]{3,2,1,0:T(8,128)}, f32[8,128]{1,0:T(8,128)S(1)}, f32[2,8,16,512]{3,2,1,0:T(8,128)S(1)}, f32[2,8,16,512]{3,2,1,0:T(8,128)S(1)}, f32[2,8,16,512]{3,2,1,0:T(8,128)S(1)}) custom-call(f32[4,512]{1,0:T(4,128)S(1)} %get-tuple-element.15.levels, s32[16,16,512]{2,1,0:T(8,128)S(1)} %copy-done, f32[8,16,16,512]{3,2,1,0:T(8,128)} %vectors.3), custom_call_target="tpu_custom_call" | custom-call | flops 5000000000 | bytes 20000000 | tf_op jit(solution)/shard_map/block/pallas_call | solution.py:330
  14.0 0.0 collective-permute-done.2.from_z_a
  14.0 0.0 collective-permute-done.3.from_z_b
  14.0 0.0 collective-permute-done.1.from_x_b
  14.0 0.0 collective-permute-done.from_x_a
  14.0 1.2 %outer.1 = (f32[8,16,16,512]{3,2,1,0:T(8,128)}, f32[2,8,16,512]{3,2,1,0:T(8,128)S(1)}, f32[16,8,128]{2,1,0:T(8,128)S(1)}) custom-call(f32[8,16,16,512]{3,2,1,0:T(8,128)} %get-tuple-element.16.applied_in, f32[8,128]{1,0:T(8,128)S(1)} %get-tuple-element.17.own, f32[2,8,16,512]{3,2,1,0:T(8,128)S(1)} %get-tuple-element.18.z_faces, ...), custom_call_target="tpu_custom_call", output_to_operand_aliasing={{0}: (0, {})} | custom-call | tf_op jit(solution)/shard_map/outer/pallas_call | solution.py:355
  15.3 19.2 %all_to_all.5 = f32[16,8,128]{2,1,0:T(8,128)S(1)} all-to-all(f32[16,8,128]{2,1,0:T(8,128)S(1)} %get-tuple-element.27), channel_id=1, replica_groups=mesh['gx'=16,'yz'=16] {'yz'}, dimensions={0} | all-to-all | bytes 131072 | tf_op jit(solution)/shard_map/all_to_all | solution.py:376
  34.5 0.8 %finish.1 = (f32[8,16,16,512]{3,2,1,0:T(8,128)}, f32[128,128]{1,0:T(8,128)}) custom-call(f32[8,16,16,512]{3,2,1,0:T(8,128)} %get-tuple-element.25.applied_in, f32[2,8,16,512]{3,2,1,0:T(8,128)S(1)} %get-tuple-element.26.x_new, f32[128,128]{1,0:T(8,128)S(1)} %bitcast.1), custom_call_target="tpu_custom_call", output_to_operand_aliasing={{0}: (0, {})} | custom-call | tf_op jit(solution)/shard_map/finish/pallas_call | solution.py:378
Async XLA Ops:
  0.6 6.1 %copy-start = (s32[16,16,512]{2,1,0:T(8,128)S(1)}, s32[16,16,512]{2,1,0:T(8,128)}, u32[]{:S(2)}) copy-start(s32[16,16,512]{2,1,0:T(8,128)} %kinds.1) | copy-start | bytes 1572868
  2.1 11.9 %collective-permute-start.2 = (f32[10,8,512]{2,1,0:T(8,128)S(1)}, f32[10,8,512]{2,1,0:T(8,128)S(1)}, u32[]{:S(2)}, u32[]{:S(2)}) collective-permute-start(f32[10,8,512]{2,1,0:T(8,128)S(1)} %get-tuple-element.21.z_a), channel_id=1, source_target_pairs={{0,1},{1,0},{2,3},{3,2},{4,5},{5,4},{6,7},{7,6},{8,9},{9,8},{10,11... | collective-permute-start | bytes 491528 | tf_op jit(solution)/shard_map/ppermute | solution.py:326
  3.7 10.2 %collective-permute-start.3 = (f32[10,8,512]{2,1,0:T(8,128)S(1)}, f32[10,8,512]{2,1,0:T(8,128)S(1)}, u32[]{:S(2)}, u32[]{:S(2)}) collective-permute-start(f32[10,8,512]{2,1,0:T(8,128)S(1)} %get-tuple-element.22.z_b), channel_id=1, source_target_pairs={{0,16},{1,2},{2,1},{3,4},{4,3},{5,6},{6,5},{7,8},{8,7},{9,10},{10,... | collective-permute-start | bytes 491528 | tf_op jit(solution)/shard_map/ppermute | solution.py:324
  3.8 10.2 %collective-permute-start.1 = (f32[9,16,512]{2,1,0:T(8,128)S(1)}, f32[9,16,512]{2,1,0:T(8,128)S(1)}, u32[]{:S(2)}, u32[]{:S(2)}) collective-permute-start(f32[9,16,512]{2,1,0:T(8,128)S(1)} %get-tuple-element.23.x_b), channel_id=1, source_target_pairs={{0,2},{1,3},{2,0},{3,1},{4,6},{5,7},{6,4},{7,5},{8,10},{9,11},{10,... | collective-permute-start | bytes 884744 | tf_op jit(solution)/shard_map/ppermute | solution.py:325
  4.7 9.3 %collective-permute-start = (f32[9,16,512]{2,1,0:T(8,128)S(1)}, f32[9,16,512]{2,1,0:T(8,128)S(1)}, u32[]{:S(2)}, u32[]{:S(2)}) collective-permute-start(f32[9,16,512]{2,1,0:T(8,128)S(1)} %get-tuple-element.24.x_a), channel_id=1, source_target_pairs={{0,16},{16,0},{32,48},{48,32},{64,80},{80,64},{96,112},{112,96},{1... | collective-permute-start | bytes 884744 | tf_op jit(solution)/shard_map/ppermute | solution.py:327

commit v6 on v5

--- a/solution.py
+++ b/solution.py
@@ -216,17 +216,19 @@
         part, at = divmod(end, half)
         x_new[side, :, 0:1, :] += z_flux[0, :, part, at : at + 1, :]
         x_new[side, :, cells_z - 1 : cells_z, :] += z_flux[1, :, part, at : at + 1, :]
-    own_z = products(split(rows(z_flux[0])), split(rows(z_faces[0])))
-    own_z += products(split(rows(z_flux[1])), split(rows(z_faces[1])))
+    lefts = [split(rows(z_flux[0])), split(rows(z_flux[1]))]
+    rights = [split(rows(z_faces[0])), split(rows(z_faces[1]))]
     for side, other in ((1 - tile_odd, from_z_a), (tile_odd, from_z_b)):
         left = split(rows(z_flux[side, :, side]))
         crosses_z.append(fold(products(left, split(rows(other[0:count]))), count, half))
-    own_x, crosses_x = 0.0, []
+    crosses_x = []
     for flux, mine, other in zip(fluxes_x, (x_a, x_b), (from_x_a, from_x_b)):
         left = split(rows(flux))
-        own_x += products(left, split(rows(mine[0:count])))
+        lefts.append(left)
+        rights.append(split(rows(mine[0:count])))
         crosses_x.append(fold(products(left, split(rows(other[0:count]))), count, cells_z))
 
+    own_outer = products(jnp.concatenate(lefts, axis=1), jnp.concatenate(rights, axis=1))
     scale = 1.0 / (cells_z * length)
     entry = lax.broadcasted_iota(jnp.int32, (width, width), 0)
     column = lax.broadcasted_iota(jnp.int32, (width, width), 1)
@@ -236,7 +238,7 @@
     place_z = ((entry & (width // 2 - 1)) >> (half.bit_length() - 1)) + tile_there * count == column
     stacked = jnp.concatenate(
         [
-            own[...] + fold(own_x, count, cells_z) + fold(own_z, count, cells_x),
+            own[...] + fold(own_outer, count, cells_z),
             -crosses_x[0],
             -crosses_x[1],
             -jnp.concatenate(crosses_z, axis=1),

time: 35.4 us -> 35.4 us (level)
  no operation moved by 1% of the time
where the time goes in v6:
time: 35.4 us; the launch traced here: 35.3 us
  blocking collectives  19.2 us (54%)
  Pallas kernels  10.7 us (30%)
  starting transfers between devices  4.61 us (13%)
  between operations  0.7 us (2%)
    all_to_all x1, blocking collectives, shards(): tile = lax.all_to_all(blocks, 'yz', split_axis=0, concat_axis=0, tiled=True)  19.2 us
    pallas_call x1, Pallas kernels, shards(): pl.pallas_call(functools.partial(block_kernel, chunks), out_shape=(pltpu....  7.26 us
    ppermute x1, starting transfers between devices, shards(): from_x_a = lax.ppermute(x_a, 'gx', [(i, i ^ 1) for i in range(slabs)])  1.99 us
    ppermute x1, starting transfers between devices, shards(): from_z_a = lax.ppermute(z_a, 'yz', [(i, i ^ 1) for i in range(tiles)])  1.68 us
    pallas_call x1, Pallas kernels, shards(): pl.pallas_call(faces_kernel, out_shape=(shape((count + 1, cells_z, length...  1.42 us
    pallas_call x1, Pallas kernels, shards(): pl.pallas_call(outer_kernel, out_shape=(pltpu.HBM(vectors.shape, F32), sh...  1.23 us
    ppermute x1, starting transfers between devices, shards(): from_x_b = lax.ppermute(x_b, both, near_x)  0.94 us
    pallas_call x1, Pallas kernels, shards(): pl.pallas_call(functools.partial(finish_kernel, count), out_shape=(pltpu....  0.83 us
  transfers between devices with their start and end apart: 4, of which 0 were waited for; matrix products, arithmetic and copies ran while one was open for 0% of the time, Pallas kernels for 21%

profile of v6, /device:TPU:6, one launch (start us, length us, event | category | flops | bytes accessed | tf_op | source)
XLA Modules:
  0.0 35.3 jit_solution(6672513523396950089)
XLA Ops:
  0.6 0.0 copy-start
  0.6 1.4 %faces.1 = (f32[9,16,512]{2,1,0:T(8,128)S(1)}, f32[9,16,512]{2,1,0:T(8,128)S(1)}, f32[10,8,512]{2,1,0:T(8,128)S(1)}, f32[10,8,512]{2,1,0:T(8,128)S(1)}, f32[4,512]{1,0:T(4,128)S(1)}) custom-call(f32[4]{0:T(128)} %table_in.1, f32[8,16,16,512]{3,2,1,0:T(8,128)} %vectors.3, s32[16,16,512]{2,1,0:T(8,128)} %kinds.1), custom_call_target="tpu_custom_call" | custom-call | tf_op jit(solution)/shard_map/faces/pallas_call | solution.py:297
  2.1 1.7 %collective-permute-start.2 = (f32[10,8,512]{2,1,0:T(8,128)S(1)}, f32[10,8,512]{2,1,0:T(8,128)S(1)}, u32[]{:S(2)}, u32[]{:S(2)}) collective-permute-start(f32[10,8,512]{2,1,0:T(8,128)S(1)} %get-tuple-element.21.z_a), channel_id=1, source_target_pairs={{0,1},{1,0},{2,3},{3,2},{4,5},{5,4},{6,7},{7,6},{8,9},{9,8},{10,11... | collective-permute-start | bytes 491528 | tf_op jit(solution)/shard_map/ppermute | solution.py:328
  3.7 0.0 collective-permute-start.3
  3.8 0.9 %collective-permute-start.1 = (f32[9,16,512]{2,1,0:T(8,128)S(1)}, f32[9,16,512]{2,1,0:T(8,128)S(1)}, u32[]{:S(2)}, u32[]{:S(2)}) collective-permute-start(f32[9,16,512]{2,1,0:T(8,128)S(1)} %get-tuple-element.23.x_b), channel_id=1, source_target_pairs={{0,2},{1,3},{2,0},{3,1},{4,6},{5,7},{6,4},{7,5},{8,10},{9,11},{10,... | collective-permute-start | bytes 884744 | tf_op jit(solution)/shard_map/ppermute | solution.py:327
  4.7 2.0 %collective-permute-start = (f32[9,16,512]{2,1,0:T(8,128)S(1)}, f32[9,16,512]{2,1,0:T(8,128)S(1)}, u32[]{:S(2)}, u32[]{:S(2)}) collective-permute-start(f32[9,16,512]{2,1,0:T(8,128)S(1)} %get-tuple-element.24.x_a), channel_id=1, source_target_pairs={{0,16},{16,0},{32,48},{48,32},{64,80},{80,64},{96,112},{112,96},{1... | collective-permute-start | bytes 884744 | tf_op jit(solution)/shard_map/ppermute | solution.py:329
  6.7 0.0 copy-done
  6.7 7.3 %block.1 = (f32[8,16,16,512]{3,2,1,0:T(8,128)}, f32[8,128]{1,0:T(8,128)S(1)}, f32[2,8,16,512]{3,2,1,0:T(8,128)S(1)}, f32[2,8,16,512]{3,2,1,0:T(8,128)S(1)}, f32[2,8,16,512]{3,2,1,0:T(8,128)S(1)}) custom-call(f32[4,512]{1,0:T(4,128)S(1)} %get-tuple-element.15.levels, s32[16,16,512]{2,1,0:T(8,128)S(1)} %copy-done, f32[8,16,16,512]{3,2,1,0:T(8,128)} %vectors.3), custom_call_target="tpu_custom_call" | custom-call | flops 5000000000 | bytes 20000000 | tf_op jit(solution)/shard_map/block/pallas_call | solution.py:332
  14.0 0.0 collective-permute-done.2.from_z_a
  14.0 0.0 collective-permute-done.3.from_z_b
  14.0 0.0 collective-permute-done.1.from_x_b
  14.0 0.0 collective-permute-done.from_x_a
  14.0 1.2 %outer.1 = (f32[8,16,16,512]{3,2,1,0:T(8,128)}, f32[2,8,16,512]{3,2,1,0:T(8,128)S(1)}, f32[16,8,128]{2,1,0:T(8,128)S(1)}) custom-call(f32[8,16,16,512]{3,2,1,0:T(8,128)} %get-tuple-element.16.applied_in, f32[8,128]{1,0:T(8,128)S(1)} %get-tuple-element.17.own, f32[2,8,16,512]{3,2,1,0:T(8,128)S(1)} %get-tuple-element.18.z_faces, ...), custom_call_target="tpu_custom_call", output_to_operand_aliasing={{0}: (0, {})} | custom-call | tf_op jit(solution)/shard_map/outer/pallas_call | solution.py:357
  15.2 19.2 %all_to_all.5 = f32[16,8,128]{2,1,0:T(8,128)S(1)} all-to-all(f32[16,8,128]{2,1,0:T(8,128)S(1)} %get-tuple-element.27), channel_id=1, replica_groups=mesh['gx'=16,'yz'=16] {'yz'}, dimensions={0} | all-to-all | bytes 131072 | tf_op jit(solution)/shard_map/all_to_all | solution.py:378
  34.4 0.8 %finish.1 = (f32[8,16,16,512]{3,2,1,0:T(8,128)}, f32[128,128]{1,0:T(8,128)}) custom-call(f32[8,16,16,512]{3,2,1,0:T(8,128)} %get-tuple-element.25.applied_in, f32[2,8,16,512]{3,2,1,0:T(8,128)S(1)} %get-tuple-element.26.x_new, f32[128,128]{1,0:T(8,128)S(1)} %bitcast.1), custom_call_target="tpu_custom_call", output_to_operand_aliasing={{0}: (0, {})} | custom-call | tf_op jit(solution)/shard_map/finish/pallas_call | solution.py:380
Async XLA Ops:
  0.6 6.1 %copy-start = (s32[16,16,512]{2,1,0:T(8,128)S(1)}, s32[16,16,512]{2,1,0:T(8,128)}, u32[]{:S(2)}) copy-start(s32[16,16,512]{2,1,0:T(8,128)} %kinds.1) | copy-start | bytes 1572868
  2.1 11.9 %collective-permute-start.2 = (f32[10,8,512]{2,1,0:T(8,128)S(1)}, f32[10,8,512]{2,1,0:T(8,128)S(1)}, u32[]{:S(2)}, u32[]{:S(2)}) collective-permute-start(f32[10,8,512]{2,1,0:T(8,128)S(1)} %get-tuple-element.21.z_a), channel_id=1, source_target_pairs={{0,1},{1,0},{2,3},{3,2},{4,5},{5,4},{6,7},{7,6},{8,9},{9,8},{10,11... | collective-permute-start | bytes 491528 | tf_op jit(solution)/shard_map/ppermute | solution.py:328
  3.7 10.2 %collective-permute-start.3 = (f32[10,8,512]{2,1,0:T(8,128)S(1)}, f32[10,8,512]{2,1,0:T(8,128)S(1)}, u32[]{:S(2)}, u32[]{:S(2)}) collective-permute-start(f32[10,8,512]{2,1,0:T(8,128)S(1)} %get-tuple-element.22.z_b), channel_id=1, source_target_pairs={{0,16},{1,2},{2,1},{3,4},{4,3},{5,6},{6,5},{7,8},{8,7},{9,10},{10,... | collective-permute-start | bytes 491528 | tf_op jit(solution)/shard_map/ppermute | solution.py:326
  3.8 10.2 %collective-permute-start.1 = (f32[9,16,512]{2,1,0:T(8,128)S(1)}, f32[9,16,512]{2,1,0:T(8,128)S(1)}, u32[]{:S(2)}, u32[]{:S(2)}) collective-permute-start(f32[9,16,512]{2,1,0:T(8,128)S(1)} %get-tuple-element.23.x_b), channel_id=1, source_target_pairs={{0,2},{1,3},{2,0},{3,1},{4,6},{5,7},{6,4},{7,5},{8,10},{9,11},{10,... | collective-permute-start | bytes 884744 | tf_op jit(solution)/shard_map/ppermute | solution.py:327
  4.7 9.3 %collective-permute-start = (f32[9,16,512]{2,1,0:T(8,128)S(1)}, f32[9,16,512]{2,1,0:T(8,128)S(1)}, u32[]{:S(2)}, u32[]{:S(2)}) collective-permute-start(f32[9,16,512]{2,1,0:T(8,128)S(1)} %get-tuple-element.24.x_a), channel_id=1, source_target_pairs={{0,16},{16,0},{32,48},{48,32},{64,80},{80,64},{96,112},{112,96},{1... | collective-permute-start | bytes 884744 | tf_op jit(solution)/shard_map/ppermute | solution.py:329

commit v7 on v6

--- a/solution.py
+++ b/solution.py
@@ -156,6 +156,7 @@
         plane(index)
         return carry
 
+    near = pltpu.make_async_copy(result.at[:, 0], x_sums.at[0], sems.at[2 * chunks])
     loads[0].wait()
     plane(0)
     for chunk in range(chunks):
@@ -163,8 +164,9 @@
             loads[chunk + 1].wait()
         lax.fori_loop(max(1, chunk * step), (chunk + 1) * step, follow, 0)
         stores[chunk].start()
+        if chunk == 0:
+            near.start()
     sides = [
-        pltpu.make_async_copy(result.at[:, 0], x_sums.at[0], sems.at[2 * chunks]),
         pltpu.make_async_copy(result.at[:, cells_x - 1], x_sums.at[1], sems.at[1 + 2 * chunks]),
         pltpu.make_async_copy(result.at[:, :, 0], z_sums.at[0], sems.at[2 + 2 * chunks]),
         pltpu.make_async_copy(result.at[:, :, cells_z - 1], z_sums.at[1], sems.at[3 + 2 * chunks]),
@@ -174,7 +176,7 @@
     for copy in sides:
         copy.start()
     own[...] = fold(total[...] + gram(cells_x - 1), count, cells_z)
-    for copy in sides + stores:
+    for copy in [near] + sides + stores:
         copy.wait()
 
 

time: 35.4 us -> 35.4 us (level)
  no operation moved by 1% of the time
where the time goes in v7:
time: 35.4 us; the launch traced here: 35.3 us
  blocking collectives  19.2 us (54%)
  Pallas kernels  10.7 us (30%)
  starting transfers between devices  4.61 us (13%)
  between operations  0.7 us (2%)
    all_to_all x1, blocking collectives, shards(): tile = lax.all_to_all(blocks, 'yz', split_axis=0, concat_axis=0, tiled=True)  19.2 us
    pallas_call x1, Pallas kernels, shards(): pl.pallas_call(functools.partial(block_kernel, chunks), out_shape=(pltpu....  7.26 us
    ppermute x1, starting transfers between devices, shards(): from_x_a = lax.ppermute(x_a, 'gx', [(i, i ^ 1) for i in range(slabs)])  1.99 us
    ppermute x1, starting transfers between devices, shards(): from_z_a = lax.ppermute(z_a, 'yz', [(i, i ^ 1) for i in range(tiles)])  1.68 us
    pallas_call x1, Pallas kernels, shards(): pl.pallas_call(faces_kernel, out_shape=(shape((count + 1, cells_z, length...  1.42 us
    pallas_call x1, Pallas kernels, shards(): pl.pallas_call(outer_kernel, out_shape=(pltpu.HBM(vectors.shape, F32), sh...  1.23 us
    ppermute x1, starting transfers between devices, shards(): from_x_b = lax.ppermute(x_b, both, near_x)  0.94 us
    pallas_call x1, Pallas kernels, shards(): pl.pallas_call(functools.partial(finish_kernel, count), out_shape=(pltpu....  0.83 us
  transfers between devices with their start and end apart: 4, of which 0 were waited for; matrix products, arithmetic and copies ran while one was open for 0% of the time, Pallas kernels for 21%

profile of v7, /device:TPU:6, one launch (start us, length us, event | category | flops | bytes accessed | tf_op | source)
XLA Modules:
  0.0 35.3 jit_solution(11637558087425939933)
XLA Ops:
  0.6 0.0 copy-start
  0.6 1.4 %faces.1 = (f32[9,16,512]{2,1,0:T(8,128)S(1)}, f32[9,16,512]{2,1,0:T(8,128)S(1)}, f32[10,8,512]{2,1,0:T(8,128)S(1)}, f32[10,8,512]{2,1,0:T(8,128)S(1)}, f32[4,512]{1,0:T(4,128)S(1)}) custom-call(f32[4]{0:T(128)} %table_in.1, f32[8,16,16,512]{3,2,1,0:T(8,128)} %vectors.3, s32[16,16,512]{2,1,0:T(8,128)} %kinds.1), custom_call_target="tpu_custom_call" | custom-call | tf_op jit(solution)/shard_map/faces/pallas_call | solution.py:299
  2.1 1.7 %collective-permute-start.2 = (f32[10,8,512]{2,1,0:T(8,128)S(1)}, f32[10,8,512]{2,1,0:T(8,128)S(1)}, u32[]{:S(2)}, u32[]{:S(2)}) collective-permute-start(f32[10,8,512]{2,1,0:T(8,128)S(1)} %get-tuple-element.21.z_a), channel_id=1, source_target_pairs={{0,1},{1,0},{2,3},{3,2},{4,5},{5,4},{6,7},{7,6},{8,9},{9,8},{10,11... | collective-permute-start | bytes 491528 | tf_op jit(solution)/shard_map/ppermute | solution.py:330
  3.7 0.0 collective-permute-start.3
  3.8 0.9 %collective-permute-start.1 = (f32[9,16,512]{2,1,0:T(8,128)S(1)}, f32[9,16,512]{2,1,0:T(8,128)S(1)}, u32[]{:S(2)}, u32[]{:S(2)}) collective-permute-start(f32[9,16,512]{2,1,0:T(8,128)S(1)} %get-tuple-element.23.x_b), channel_id=1, source_target_pairs={{0,2},{1,3},{2,0},{3,1},{4,6},{5,7},{6,4},{7,5},{8,10},{9,11},{10,... | collective-permute-start | bytes 884744 | tf_op jit(solution)/shard_map/ppermute | solution.py:329
  4.7 2.0 %collective-permute-start = (f32[9,16,512]{2,1,0:T(8,128)S(1)}, f32[9,16,512]{2,1,0:T(8,128)S(1)}, u32[]{:S(2)}, u32[]{:S(2)}) collective-permute-start(f32[9,16,512]{2,1,0:T(8,128)S(1)} %get-tuple-element.24.x_a), channel_id=1, source_target_pairs={{0,16},{16,0},{32,48},{48,32},{64,80},{80,64},{96,112},{112,96},{1... | collective-permute-start | bytes 884744 | tf_op jit(solution)/shard_map/ppermute | solution.py:331
  6.7 0.0 copy-done
  6.7 7.3 %block.1 = (f32[8,16,16,512]{3,2,1,0:T(8,128)}, f32[8,128]{1,0:T(8,128)S(1)}, f32[2,8,16,512]{3,2,1,0:T(8,128)S(1)}, f32[2,8,16,512]{3,2,1,0:T(8,128)S(1)}, f32[2,8,16,512]{3,2,1,0:T(8,128)S(1)}) custom-call(f32[4,512]{1,0:T(4,128)S(1)} %get-tuple-element.15.levels, s32[16,16,512]{2,1,0:T(8,128)S(1)} %copy-done, f32[8,16,16,512]{3,2,1,0:T(8,128)} %vectors.3), custom_call_target="tpu_custom_call" | custom-call | flops 5000000000 | bytes 20000000 | tf_op jit(solution)/shard_map/block/pallas_call | solution.py:334
  14.0 0.0 collective-permute-done.2.from_z_a
  14.0 0.0 collective-permute-done.3.from_z_b
  14.0 0.0 collective-permute-done.1.from_x_b
  14.0 0.0 collective-permute-done.from_x_a
  14.0 1.2 %outer.1 = (f32[8,16,16,512]{3,2,1,0:T(8,128)}, f32[2,8,16,512]{3,2,1,0:T(8,128)S(1)}, f32[16,8,128]{2,1,0:T(8,128)S(1)}) custom-call(f32[8,16,16,512]{3,2,1,0:T(8,128)} %get-tuple-element.16.applied_in, f32[8,128]{1,0:T(8,128)S(1)} %get-tuple-element.17.own, f32[2,8,16,512]{3,2,1,0:T(8,128)S(1)} %get-tuple-element.18.z_faces, ...), custom_call_target="tpu_custom_call", output_to_operand_aliasing={{0}: (0, {})} | custom-call | tf_op jit(solution)/shard_map/outer/pallas_call | solution.py:359
  15.2 19.2 %all_to_all.5 = f32[16,8,128]{2,1,0:T(8,128)S(1)} all-to-all(f32[16,8,128]{2,1,0:T(8,128)S(1)} %get-tuple-element.27), channel_id=1, replica_groups=mesh['gx'=16,'yz'=16] {'yz'}, dimensions={0} | all-to-all | bytes 131072 | tf_op jit(solution)/shard_map/all_to_all | solution.py:380
  34.4 0.8 %finish.1 = (f32[8,16,16,512]{3,2,1,0:T(8,128)}, f32[128,128]{1,0:T(8,128)}) custom-call(f32[8,16,16,512]{3,2,1,0:T(8,128)} %get-tuple-element.25.applied_in, f32[2,8,16,512]{3,2,1,0:T(8,128)S(1)} %get-tuple-element.26.x_new, f32[128,128]{1,0:T(8,128)S(1)} %bitcast.1), custom_call_target="tpu_custom_call", output_to_operand_aliasing={{0}: (0, {})} | custom-call | tf_op jit(solution)/shard_map/finish/pallas_call | solution.py:382
Async XLA Ops:
  0.6 6.1 %copy-start = (s32[16,16,512]{2,1,0:T(8,128)S(1)}, s32[16,16,512]{2,1,0:T(8,128)}, u32[]{:S(2)}) copy-start(s32[16,16,512]{2,1,0:T(8,128)} %kinds.1) | copy-start | bytes 1572868
  2.1 11.9 %collective-permute-start.2 = (f32[10,8,512]{2,1,0:T(8,128)S(1)}, f32[10,8,512]{2,1,0:T(8,128)S(1)}, u32[]{:S(2)}, u32[]{:S(2)}) collective-permute-start(f32[10,8,512]{2,1,0:T(8,128)S(1)} %get-tuple-element.21.z_a), channel_id=1, source_target_pairs={{0,1},{1,0},{2,3},{3,2},{4,5},{5,4},{6,7},{7,6},{8,9},{9,8},{10,11... | collective-permute-start | bytes 491528 | tf_op jit(solution)/shard_map/ppermute | solution.py:330
  3.7 10.2 %collective-permute-start.3 = (f32[10,8,512]{2,1,0:T(8,128)S(1)}, f32[10,8,512]{2,1,0:T(8,128)S(1)}, u32[]{:S(2)}, u32[]{:S(2)}) collective-permute-start(f32[10,8,512]{2,1,0:T(8,128)S(1)} %get-tuple-element.22.z_b), channel_id=1, source_target_pairs={{0,16},{1,2},{2,1},{3,4},{4,3},{5,6},{6,5},{7,8},{8,7},{9,10},{10,... | collective-permute-start | bytes 491528 | tf_op jit(solution)/shard_map/ppermute | solution.py:328
  3.8 10.2 %collective-permute-start.1 = (f32[9,16,512]{2,1,0:T(8,128)S(1)}, f32[9,16,512]{2,1,0:T(8,128)S(1)}, u32[]{:S(2)}, u32[]{:S(2)}) collective-permute-start(f32[9,16,512]{2,1,0:T(8,128)S(1)} %get-tuple-element.23.x_b), channel_id=1, source_target_pairs={{0,2},{1,3},{2,0},{3,1},{4,6},{5,7},{6,4},{7,5},{8,10},{9,11},{10,... | collective-permute-start | bytes 884744 | tf_op jit(solution)/shard_map/ppermute | solution.py:329
  4.7 9.3 %collective-permute-start = (f32[9,16,512]{2,1,0:T(8,128)S(1)}, f32[9,16,512]{2,1,0:T(8,128)S(1)}, u32[]{:S(2)}, u32[]{:S(2)}) collective-permute-start(f32[9,16,512]{2,1,0:T(8,128)S(1)} %get-tuple-element.24.x_a), channel_id=1, source_target_pairs={{0,16},{16,0},{32,48},{48,32},{64,80},{80,64},{96,112},{112,96},{1... | collective-permute-start | bytes 884744 | tf_op jit(solution)/shard_map/ppermute | solution.py:331
